TPU v7x, 128 devices: a whole 4x4x4 slice. The times are simulated.
128 devices in a mesh: dap: 64 (over z_hi, y, x, core), dp: 2 (over z_lo).
Axes of the slice: x: 4, y: 4, z: 4 (z_hi: 2, z_lo: 2; z = z_hi * 2 + z_lo), core: 2. Of those that a mesh axis runs over, the one named last changes fastest.
Arguments:
- pair: bfloat16 [1536, 768, 128], P(('dp', 'dap')), parts along dimension 0, may hold values from -6 to 6
- pair_mask: int32 [1536, 768], P('dp', 'dap'), parts along dimension 0, may hold values 0 or 1
- ln_gain: float32 [128], replicated, may hold values from 0.1 to 1.9
- ln_offset: float32 [128], replicated, may hold values from -3 to 3
- bias_weight: bfloat16 [128, 4], replicated, may hold values from -14.142136 to 14.142136
- query_weight: bfloat16 [128, 128], replicated, may hold values from -2.4748737 to 2.4748737
- key_weight: bfloat16 [128, 128], replicated, may hold values from -2.4748737 to 2.4748737
- value_weight: bfloat16 [128, 128], replicated, may hold values from -0.5 to 0.5
- gate_weight: bfloat16 [128, 128], replicated, may hold values from -0.5 to 0.5
- gate_offset: float32 [128], replicated, may hold values from -4 to 4
- out_weight: bfloat16 [128, 128], replicated, may hold values from -0.5 to 0.5
- out_offset: float32 [128], replicated, may hold values from -3 to 3
Outputs:
- update: bfloat16 [1536, 768, 128], P(('dp', 'dap')), parts along dimension 0
There are 2 independent parts, one for each index of `dp`. A program takes and returns all parts, laid end to end along the dimension named above; an argument that names none is the same for every part. Nothing has to cross between parts.
All inputs are finite; a program needn't handle non-finite values. No bound on the sum of `pair_mask` on one device may be relied on, other than what follows from the above.
Results may differ from a plain program's by a relative error of at most 0.014.
The roundings to bfloat16 on the way count: a program that leaves them out, or rounds other values in their place, can miss the bound.
Values may be sent and summed in bfloat16 or wider, within the bound.
No kernel may reach another device: no remote copies, remote signals or barrier semaphores. Data moves between devices by JAX's collectives and lax.ppermute only.
A program may use at most 128 MiB of HBM per device.

v0:
```python
import functools

import jax
import jax.numpy as jnp
from jax import lax
from jax.experimental import pallas as pl
from jax.experimental.pallas import tpu as pltpu
from jax.sharding import PartitionSpec as P

NEG_BIG = 1000000000.0
EPSILON = 1e-05
CHUNKS = 2
ATTEND_MIB = 40
TURN_MIB = 60
FINISH_MIB = 30
TOTAL_LOW = 1e-20
TOTAL_HIGH = 1e30
NT = (((1,), (1,)), ((), ()))
PLACE = ("z", "y", "x", "core")
PLACE_SIZES = (2, 4, 4, 2)
TOTAL = 64
FIRST = 8
SHIFTS = (0, 1, 2, 3)


def dot(lhs, rhs):
    return jnp.dot(lhs, rhs, preferred_element_type=jnp.float32)


def dot_nt(lhs, rhs):
    return lax.dot_general(lhs, rhs, NT, preferred_element_type=jnp.float32)


def in_vmem(count):
    return [pl.BlockSpec(memory_space=pltpu.VMEM)] * count


def norm_kernel(rows, width, heads, pair_ref, gain_ref, offset_ref, bias_weight_ref, normed_ref, bias_ref, wide_ref):
    weight = bias_weight_ref[...]
    blank = jnp.zeros_like(weight)
    both = jnp.concatenate(
        [jnp.concatenate([weight, blank], axis=1), jnp.concatenate([blank, weight], axis=1)], axis=0
    )
    for row in range(rows):
        wide = pair_ref[pl.ds(row * width, width), :].astype(jnp.float32)
        centred = wide - jnp.mean(wide, axis=1, keepdims=True)
        spread = jnp.mean(centred * centred, axis=1, keepdims=True)
        normed = centred * lax.rsqrt(spread + EPSILON) * gain_ref[...] + offset_ref[...]
        normed_ref[pl.ds(row * width, width), :] = normed.astype(jnp.bfloat16)
        if row % 2:
            two = [normed_ref[pl.ds(at * width, width), :] for at in (row - 1, row)]
            wide_ref[pl.ds((row - 1) * heads, 2 * heads), :] = dot_nt(both, jnp.concatenate(two, axis=1))
    for copy in range(bias_ref.shape[0] // (rows * heads)):
        bias_ref[pl.ds(copy * rows * heads, rows * heads), :] = wide_ref[...].astype(jnp.bfloat16)


def layout_kernel(rows, width, groups, chunks, normed_ref, mask_ref, *refs):
    weight_refs, chunk_refs = refs[:4], refs[4 : 4 + chunks]
    present_ref, packed_ref, wide_ref = refs[4 + chunks : 7 + chunks]
    staged_refs = refs[7 + chunks :]
    cols = width // groups
    per = cols // chunks
    for row in range(rows):
        wide_ref[row % 2] = normed_ref[pl.ds(row * width, width), :].astype(jnp.float32)
        for col in range(cols):
            chunk, place = divmod(col, per)
            staged_refs[chunk][pl.ds(row * per + place, groups, stride=rows * per), :] = wide_ref[
                row % 2, pl.ds(col, groups, stride=cols), :
            ]
    for chunk in range(chunks):
        chunk_refs[chunk][...] = staged_refs[chunk][...].astype(jnp.bfloat16)
    present_ref[...] = mask_ref[...].astype(jnp.float32).T.astype(jnp.bfloat16)
    channels = normed_ref.shape[1]
    for at, ref in enumerate(weight_refs):
        packed_ref[:, at * channels : (at + 1) * channels] = ref[...]


def hold_kernel(*refs):
    pass


def hold(*arrays):
    whole = [pl.BlockSpec(memory_space=pl.ANY)] * len(arrays)
    return pl.pallas_call(
        hold_kernel,
        out_shape=[jax.ShapeDtypeStruct(one.shape, one.dtype) for one in arrays],
        in_specs=whole,
        out_specs=whole,
        input_output_aliases={at: at for at in range(len(arrays))},
        name="hold",
    )(*arrays)


def place_of(index):
    place = {}
    for axis, size in zip(reversed(PLACE), reversed(PLACE_SIZES)):
        place[axis] = index % size if isinstance(index, int) else lax.rem(index, size)
        index = index // size
    return place


def index_of(place):
    index = 0
    for axis, size in zip(PLACE, PLACE_SIZES):
        index = index * size + place[axis]
    return index


ORDER = (("y", "x"), ("x", "y"))


def first_groups():
    groups = {}
    for index in range(TOTAL):
        place = place_of(index)
        groups.setdefault((place["core"], place[ORDER[place["core"]][1]]), []).append(index)
    return list(groups.values())


def second_pairs(step):
    pairs = []
    for index in range(TOTAL):
        place = place_of(index)
        axis = ORDER[place["core"]][1]
        pairs.append((index, index_of({**place, axis: (place[axis] + step) % 4})))
    return pairs


def gather_bias(bias_copies, sends):
    first = lax.all_to_all(
        bias_copies.reshape((FIRST, bias_copies.shape[0] // FIRST, bias_copies.shape[1])),
        "dap",
        split_axis=0,
        concat_axis=0,
        axis_index_groups=first_groups(),
        tiled=True,
    ).reshape(bias_copies.shape)
    first, *sends = hold(first, *sends)
    pieces = [first if step == 0 else lax.ppermute(first, "dap", second_pairs(step)) for step in SHIFTS]
    other_core = [(index, index ^ 1) for index in range(TOTAL)]
    return pieces + [lax.ppermute(piece, "dap", other_core) for piece in pieces], sends


def turn_kernel(heads, rows, handed, *refs):
    count = 2 * len(SHIFTS)
    pieces, turned_ref, wide_ref = refs[:count], refs[count + handed], refs[-1]
    width = turned_ref.shape[1]
    tile = wide_ref.shape[2]
    here = place_of(lax.axis_index("dap"))
    block = rows * heads

    for other in range(2):
        core = here["core"] if other == 0 else 1 - here["core"]
        last = jnp.where(core == 0, here["x"], here["y"])
        for far, step in enumerate(SHIFTS):
            second = lax.rem(last + 4 - step, 4)
            for place in range(FIRST):
                first = place % 4
                at = {
                    "z": place // 4,
                    "y": jnp.where(core == 0, first, second),
                    "x": jnp.where(core == 0, second, first),
                    "core": core,
                }
                start = pl.multiple_of(index_of(at) * block, 16)
                for lane in range(width // tile):
                    wide_ref[lane, pl.ds(start, block), :] = pieces[other * len(SHIFTS) + far][
                        pl.ds(place * block, block), lane * tile : (lane + 1) * tile
                    ].astype(jnp.float32)

    unit = (
        lax.broadcasted_iota(jnp.int32, (tile, tile), 0) == lax.broadcasted_iota(jnp.int32, (tile, tile), 1)
    ).astype(jnp.bfloat16)
    for head in range(heads):
        for at in range(0, width, tile):
            one = wide_ref[at // tile, pl.ds(head, width, stride=heads), :].astype(jnp.bfloat16)
            turned_ref[head, pl.ds(at, tile), :] = dot_nt(unit, one).astype(jnp.bfloat16)


def attend_kernel(
    chunk,
    per,
    heads,
    moved_ref,
    bias_ref,
    present_ref,
    weight_ref,
    gate_offset_ref,
    out_ref,
    source_ref,
    result_ref,
    fine_ref,
    *sets,
):
    channels = moved_ref.shape[1]
    width, mask_cols = present_ref.shape
    head_dim = channels // heads
    source_ref[...] = moved_ref[...].astype(jnp.float32)
    lane_head = lax.broadcasted_iota(jnp.int32, (1, channels), 1) // head_dim
    own = [(lane_head == head).astype(jnp.bfloat16) for head in range(heads)]
    fine_ref[...] = jnp.ones_like(fine_ref)
    share = width // heads
    first_set, second_set = sets[:5], sets[5:]

    def project(col, part, buffers, hide=True):
        query_ref, key_ref, value_ref, gate_ref, _ = buffers
        rows = pl.ds(part * share, share)
        source = source_ref[pl.ds(col + part * share * per, share, stride=per), :].astype(jnp.bfloat16)
        wide = dot(source, weight_ref[...])
        query_ref[rows, :] = (wide[:, :channels] * head_dim ** (-0.5)).astype(jnp.bfloat16)
        key_ref[rows, :] = wide[:, channels : 2 * channels].astype(jnp.bfloat16)
        pick = (lax.broadcasted_iota(jnp.int32, (mask_cols, channels), 0) == chunk * per + col).astype(jnp.bfloat16)
        present = dot(present_ref[rows, :], pick).astype(jnp.bfloat16)
        values = wide[:, 2 * channels : 3 * channels].astype(jnp.bfloat16)
        value_ref[rows, :channels] = values * present if hide else values
        value_ref[rows, channels:] = present
        gate_ref[rows, :] = jax.nn.sigmoid(wide[:, 3 * channels :] + gate_offset_ref[...]).astype(jnp.bfloat16)

    def attend(head, buffers):
        query_ref, key_ref, value_ref, _, total_ref = buffers
        scores = dot_nt(query_ref[...] * own[head], key_ref[...]) + bias_ref[head].astype(jnp.float32)
        total = dot(jnp.exp(scores).astype(jnp.bfloat16), value_ref[...])
        for low in (head * head_dim, channels + head * head_dim):
            total_ref[:, low : low + head_dim] = total[:, low : low + head_dim]

    def close(col, buffers):
        _, _, _, gate_ref, total_ref = buffers
        sums = total_ref[:, channels:]
        fine = jnp.where((sums > TOTAL_LOW) & (sums < TOTAL_HIGH), 1.0, 0.0)
        fine_ref[...] = jnp.minimum(fine_ref[...], jnp.min(fine.reshape(width // 8, 8, channels), axis=0))
        result_ref[pl.ds(col, width, stride=per), :] = (
            total_ref[:, :channels] / sums * gate_ref[...].astype(jnp.float32)
        )

    for part in range(heads):
        project(0, part, first_set)

    def two_columns(step, carry):
        for now, later, col in ((first_set, second_set, 2 * step), (second_set, first_set, 2 * step + 1)):
            for head in range(heads):
                attend(head, now)
                project(jnp.minimum(col + 1, per - 1), head, later)
            close(col, now)
        return carry

    lax.fori_loop(0, per // 2, two_columns, 0)

    @pl.when(jnp.min(fine_ref[...]) < 0.5)
    def _():
        tile = 128
        query_ref, key_ref, value_ref, gate_ref, total_ref = first_set

        def exact(col, carry):
            for part in range(heads):
                project(col, part, first_set, hide=False)
            first = (lax.broadcasted_iota(jnp.int32, (8, channels), 1) == 0).astype(jnp.bfloat16)
            lift = NEG_BIG * (dot_nt(first, value_ref[:, channels:])[:1] - 1.0)

            def rows_exact(step, inner):
                rows = pl.ds(pl.multiple_of(step * tile, tile), tile)
                for head in range(heads):
                    low = head * head_dim
                    scores = dot_nt(query_ref[rows, :] * own[head], key_ref[...])
                    scores = scores + bias_ref[head, rows, :].astype(jnp.float32) + lift
                    probs = jnp.exp(scores - jnp.max(scores, axis=1, keepdims=True))
                    totals = jnp.sum(probs, axis=1, keepdims=True)
                    attended = dot(probs.astype(jnp.bfloat16), value_ref[:, :channels]) / totals
                    total_ref[rows, low : low + head_dim] = attended[:, low : low + head_dim]
                return inner

            lax.fori_loop(0, width // tile, rows_exact, 0)
            result_ref[pl.ds(col, width, stride=per), :] = total_ref[:, :channels] * gate_ref[...].astype(jnp.float32)
            return carry

        lax.fori_loop(0, per, exact, 0)

    out_ref[...] = result_ref[...].astype(jnp.bfloat16)


def finish_kernel(rows, width, groups, chunks, *refs):
    chunk_refs = refs[:chunks]
    out_weight_ref, out_offset_ref, update_ref = refs[chunks : chunks + 3]
    wide_refs = refs[chunks + 3 : 2 * chunks + 3]
    row_ref = refs[2 * chunks + 3]
    cols = width // groups
    per = cols // chunks
    for chunk in range(chunks):
        wide_refs[chunk][...] = dot(chunk_refs[chunk][...], out_weight_ref[...]) + out_offset_ref[...]
    for row in range(rows):
        for col in range(cols):
            chunk, place = divmod(col, per)
            row_ref[row % 2, pl.ds(col, groups, stride=cols), :] = wide_refs[chunk][
                pl.ds(row * per + place, groups, stride=rows * per), :
            ]
        update_ref[pl.ds(row * width, width), :] = row_ref[row % 2].astype(jnp.bfloat16)


def local(
    pair,
    pair_mask,
    ln_gain,
    ln_offset,
    bias_weight,
    query_weight,
    key_weight,
    value_weight,
    gate_weight,
    gate_offset,
    out_weight,
    out_offset,
):
    rows, width, channels = pair.shape
    groups = lax.axis_size("dap")
    cols = width // groups
    per = cols // CHUNKS
    heads = bias_weight.shape[1]
    block = groups * rows * per
    low, wide = jnp.bfloat16, jnp.float32
    params = pltpu.CompilerParams(vmem_limit_bytes=60 * 1024 * 1024)
    normed, bias_copies = pl.pallas_call(
        functools.partial(norm_kernel, rows, width, heads),
        out_shape=[
            jax.ShapeDtypeStruct((rows * width, channels), low),
            jax.ShapeDtypeStruct((FIRST * rows * heads, width), low),
        ],
        in_specs=in_vmem(4),
        out_specs=in_vmem(2),
        scratch_shapes=[pltpu.VMEM((rows * heads, width), wide)],
        compiler_params=params,
        name="norm",
    )(pair.reshape(rows * width, channels), ln_gain.reshape(1, channels), ln_offset.reshape(1, channels), bias_weight.T)
    *sends, present, packed = pl.pallas_call(
        functools.partial(layout_kernel, rows, width, groups, CHUNKS),
        out_shape=[jax.ShapeDtypeStruct((block, channels), low)] * CHUNKS
        + [jax.ShapeDtypeStruct((width, cols), low), jax.ShapeDtypeStruct((channels, 4 * channels), low)],
        in_specs=in_vmem(6),
        out_specs=in_vmem(CHUNKS + 2),
        scratch_shapes=[pltpu.VMEM((2, width, channels), wide)] + [pltpu.VMEM((block, channels), wide)] * CHUNKS,
        compiler_params=params,
        cost_estimate=pl.CostEstimate(flops=10**6, bytes_accessed=15 * 10**6, transcendentals=0),
        name="layout",
    )(normed, pair_mask.T, query_weight, key_weight, value_weight, gate_weight)

    pieces, sends = gather_bias(bias_copies, sends)
    whole = pl.BlockSpec(memory_space=pl.ANY)
    later = sends[1:]
    turned, *later = pl.pallas_call(
        functools.partial(turn_kernel, heads, rows, len(later)),
        out_shape=[jax.ShapeDtypeStruct((heads, width, width), low)]
        + [jax.ShapeDtypeStruct(one.shape, one.dtype) for one in later],
        in_specs=in_vmem(len(pieces)) + [whole] * len(later),
        out_specs=in_vmem(1) + [whole] * len(later),
        input_output_aliases={len(pieces) + at: 1 + at for at in range(len(later))},
        scratch_shapes=[pltpu.VMEM((width // channels, width * heads, channels), wide)],
        compiler_params=pltpu.CompilerParams(vmem_limit_bytes=TURN_MIB * 1024 * 1024),
        name="turn",
    )(*pieces, *later)
    moved = [
        lax.all_to_all(
            send.reshape(groups, rows * per, channels), "dap", split_axis=0, concat_axis=0, tiled=True
        ).reshape(block, channels)
        for send in (sends[0], *later)
    ]

    returned = []
    for chunk in range(CHUNKS):
        gated = pl.pallas_call(
            functools.partial(attend_kernel, chunk, per, heads),
            out_shape=jax.ShapeDtypeStruct((block, channels), low),
            in_specs=in_vmem(5),
            out_specs=in_vmem(1)[0],
            scratch_shapes=[
                pltpu.VMEM((block, channels), wide),
                pltpu.VMEM((block, channels), wide),
                pltpu.VMEM((8, channels), wide),
            ]
            + 2
            * [
                pltpu.VMEM((width, channels), low),
                pltpu.VMEM((width, channels), low),
                pltpu.VMEM((width, 2 * channels), low),
                pltpu.VMEM((width, channels), low),
                pltpu.VMEM((width, 2 * channels), wide),
            ],
            compiler_params=pltpu.CompilerParams(vmem_limit_bytes=ATTEND_MIB * 1024 * 1024),
            cost_estimate=pl.CostEstimate(
                flops=per * heads * width * width * channels * 6,
                bytes_accessed=2 * heads * width * width,
                transcendentals=per * heads * width * width,
            ),
            name="attend",
        )(
            moved[chunk],
            turned,
            present,
            packed,
            gate_offset.reshape(1, channels),
        )
        returned.append(
            lax.all_to_all(
                gated.reshape(groups, rows * per, channels), "dap", split_axis=0, concat_axis=0, tiled=True
            ).reshape(block, channels)
        )
    update = pl.pallas_call(
        functools.partial(finish_kernel, rows, width, groups, CHUNKS),
        out_shape=jax.ShapeDtypeStruct((rows * width, channels), low),
        in_specs=in_vmem(CHUNKS + 2),
        out_specs=in_vmem(1)[0],
        scratch_shapes=[pltpu.VMEM((block, channels), wide)] * CHUNKS + [pltpu.VMEM((2, width, channels), wide)],
        compiler_params=pltpu.CompilerParams(vmem_limit_bytes=FINISH_MIB * 1024 * 1024),
        name="finish",
    )(*returned, out_weight, out_offset.reshape(1, channels))
    return update.reshape(rows, width, channels)


def solution(mesh):
    in_specs = (P(("dp", "dap"), None, None), P("dp", "dap")) + (P(),) * 10
    out_specs = P(("dp", "dap"), None, None)
    return jax.shard_map(local, mesh=mesh, in_specs=in_specs, out_specs=out_specs, check_vma=False)
```

profile of v0, /device:TPU:1, one launch (start us, length us, event | category | flops | bytes accessed | tf_op | source)
XLA Modules:
  0.0 267.9 jit_solution(17517395125895549167)
XLA Ops:
  0.0 6.0 %norm.1 = (bf16[9216,128]{1,0:T(8,128)(2,1)}, bf16[384,768]{1,0:T(8,128)(2,1)}) custom-call(bf16[9216,128]{1,0:T(8,128)(2,1)} %bitcast.29, f32[1,128]{1,0:T(1,128)} %bitcast.33, f32[1,128]{1,0:T(1,128)} %bitcast.34, bf16[4,128]{1,0:T(4,128)(2,1)} %bitcast.32), custom_call_target="tpu_custom_call" | custom-call | tf_op jit(solution)/shard_map/norm/pallas_call | solution.py:320
  6.0 8.2 %all-to-all-start = ((bf16[8,48,768]{2,1,0:T(8,128)(2,1)}), bf16[8,48,768]{2,1,0:T(8,128)(2,1)S(1)}, u32[]{:S(2)}, u32[]{:S(2)}) async-start(bf16[8,48,768]{2,1,0:T(8,128)(2,1)} %bitcast.30), calls=%async_computation | async-start | bytes 1179648 | tf_op jit(solution)/shard_map/all_to_all | solution.py:130
  14.1 4.6 %layout.1 = (bf16[4608,128]{1,0:T(8,128)(2,1)}, bf16[4608,128]{1,0:T(8,128)(2,1)}, bf16[768,12]{1,0:T(8,128)(2,1)}, bf16[128,512]{1,0:T(8,128)(2,1)}) custom-call(bf16[9216,128]{1,0:T(8,128)(2,1)} %get-tuple-element.17.normed_ref, s32[12,768]{1,0:T(8,128)} %bitcast.31, bf16[128,128]{1,0:T(8,128)(2,1)} %refs_0_.1, bf16[128,128]{1,0:T(8,128)(2,1)} %refs_1_.1, ...), custom_call_target="tpu_custom_call" | custom-call | flops 1000000 | bytes 15000000 | tf_op jit(solution)/shard_map/layout/pallas_call | solution.py:332
  18.7 5.6 %all-to-all-done = bf16[8,48,768]{2,1,0:T(8,128)(2,1)S(1)} async-done(((bf16[8,48,768]{2,1,0:T(8,128)(2,1)}), bf16[8,48,768]{2,1,0:T(8,128)(2,1)S(1)}, u32[]{:S(2)}, u32[]{:S(2)}) %all-to-all-start) | async-done | bytes 589856 | tf_op jit(solution)/shard_map/all_to_all | solution.py:130
  24.3 0.0 copy-start.9
  24.3 0.8 copy-done.9
  25.1 3.0 %collective-permute-start.2 = (bf16[384,768]{1,0:T(8,128)(2,1)}, bf16[384,768]{1,0:T(8,128)(2,1)S(1)}, u32[]{:S(2)}, u32[]{:S(2)}) collective-permute-start(bf16[384,768]{1,0:T(8,128)(2,1)} %get-tuple-element.21.refs_0_), channel_id=1, source_target_pairs={{0,12},{2,50},{4,0},{6,54},{8,4},{10,58},{12,8},{14,62},{16,28},{1... | collective-permute-start | bytes 1769480 | tf_op jit(solution)/shard_map/ppermute | solution.py:139
  28.1 0.2 collective-permute-start.1
  28.4 0.7 collective-permute-start
  29.0 0.0 copy-start.10
  29.0 9.0 %all-to-all-start.1 = ((bf16[64,72,128]{2,1,0:T(8,128)(2,1)}), bf16[64,72,128]{2,1,0:T(8,128)(2,1)S(1)}, u32[]{:S(2)}, u32[]{:S(2)}) async-start(bf16[64,72,128]{2,1,0:T(8,128)(2,1)} %bitcast.28), calls=%async_computation.1 | async-start | bytes 2359296 | tf_op jit(solution)/shard_map/all_to_all | solution.py:359
  38.0 0.0 copy-done.10
  38.1 0.5 collective-permute-start.3
  38.6 7.2 %collective-permute-done.2.refs_3_ = bf16[384,768]{1,0:T(8,128)(2,1)S(1)} collective-permute-done((bf16[384,768]{1,0:T(8,128)(2,1)}, bf16[384,768]{1,0:T(8,128)(2,1)S(1)}, u32[]{:S(2)}, u32[]{:S(2)}) %collective-permute-start.2) | collective-permute-done | bytes 589856 | tf_op jit(solution)/shard_map/ppermute | solution.py:139
  45.7 0.0 copy-start.11
  45.8 0.0 collective-permute-start.6
  45.8 0.0 collective-permute-done.1.refs_2_
  45.8 0.0 copy-start.12
  45.8 0.5 collective-permute-start.5
  46.3 4.5 %collective-permute-done.refs_1_ = bf16[384,768]{1,0:T(8,128)(2,1)S(1)} collective-permute-done((bf16[384,768]{1,0:T(8,128)(2,1)}, bf16[384,768]{1,0:T(8,128)(2,1)S(1)}, u32[]{:S(2)}, u32[]{:S(2)}) %collective-permute-start) | collective-permute-done | bytes 589856 | tf_op jit(solution)/shard_map/ppermute | solution.py:139
  50.8 0.0 copy-start.13
  50.8 3.0 %collective-permute-start.4 = (bf16[384,768]{1,0:T(8,128)(2,1)S(1)}, bf16[384,768]{1,0:T(8,128)(2,1)S(1)}, u32[]{:S(2)}, u32[]{:S(2)}) collective-permute-start(bf16[384,768]{1,0:T(8,128)(2,1)S(1)} %collective-permute-done.refs_1_), channel_id=1, source_target_pairs={{0,2},{2,0},{4,6},{6,4},{8,10},{10,8},{12,14},{14,12},{16,18},{18,... | collective-permute-start | bytes 1769480 | tf_op jit(solution)/shard_map/ppermute | solution.py:141
  53.8 0.0 collective-permute-done.3.refs_4_
  53.8 0.0 copy-start.14
  53.8 0.0 collective-permute-done.6.refs_7_
  53.8 0.0 copy-start.15
  53.8 0.0 collective-permute-done.5.refs_6_
  53.8 0.0 copy-start.16
  53.9 1.6 collective-permute-done.4.refs_5_
  55.4 0.0 copy-done.14
  55.5 0.0 copy-done.15
  55.5 0.0 copy-done.16
  55.5 0.0 copy-start.17
  55.5 0.8 copy-done.17
  56.3 0.0 copy-done.11
  56.3 0.0 copy-done.12
  56.3 0.0 copy-done.13
  56.3 6.5 %turn.1 = (bf16[4,768,768]{2,1,0:T(8,128)(2,1)}, bf16[4608,128]{1,0:T(8,128)(2,1)}) custom-call(bf16[384,768]{1,0:T(8,128)(2,1)} %get-tuple-element.21.refs_0_, bf16[384,768]{1,0:T(8,128)(2,1)} %copy-done.13, bf16[384,768]{1,0:T(8,128)(2,1)} %copy-done.12, bf16[384,768]{1,0:T(8,128)(2,1)} %copy-done.11, ...), custom_call_target="tpu_custom_call", output_to_operand_aliasing={{1}: (8, {})} | custom-call | tf_op jit(solution)/shard_map/turn/pallas_call | solution.py:347
  62.8 0.0 all-to-all-done.1
  62.8 0.0 copy-start.4
  62.8 0.0 copy-start.6
  62.8 0.0 copy-start.8
  62.8 5.8 %all-to-all-start.3 = ((bf16[64,72,128]{2,1,0:T(8,128)(2,1)}), bf16[64,72,128]{2,1,0:T(8,128)(2,1)S(1)}, u32[]{:S(2)}, u32[]{:S(2)}) async-start(bf16[64,72,128]{2,1,0:T(8,128)(2,1)} %bitcast.26), calls=%async_computation.3 | async-start | bytes 2359296 | tf_op jit(solution)/shard_map/all_to_all | solution.py:359
  68.6 0.0 copy-done.4
  68.6 0.0 copy-done.6
  68.6 0.0 copy-done.8
  68.6 0.0 copy-start.2
  68.6 2.3 copy-done.2
  71.0 75.0 %attend.2 = bf16[4608,128]{1,0:T(8,128)(2,1)} custom-call(bf16[4608,128]{1,0:T(8,128)(2,1)S(1)} %bitcast.20, bf16[4,768,768]{2,1,0:T(8,128)(2,1)S(1)} %copy-done.2, bf16[768,12]{1,0:T(8,128)(2,1)S(1)} %copy-done.4, bf16[128,512]{1,0:T(8,128)(2,1)S(1)} %copy-done.6, f32[1,128]{1,0:T(1,128)S(1)} %bitcast.24), custom_call_target="tpu_custom_call" | custom-call | flops 10871635968 | bytes 4718592 | tf_op jit(solution)/shard_map/attend/pallas_call | solution.py:367
  146.0 0.0 all-to-all-done.3
  146.0 10.4 %all-to-all-start.2 = ((bf16[64,72,128]{2,1,0:T(8,128)(2,1)}), bf16[64,72,128]{2,1,0:T(8,128)(2,1)S(1)}, u32[]{:S(2)}, u32[]{:S(2)}) async-start(bf16[64,72,128]{2,1,0:T(8,128)(2,1)} %bitcast.10), calls=%async_computation.2 | async-start | bytes 2359296 | tf_op jit(solution)/shard_map/all_to_all | solution.py:400
  156.4 0.0 copy-start.3
  156.4 2.3 copy-done.3
  158.7 0.0 copy-start.5
  158.7 0.9 copy-done.5
  159.6 0.9 copy-done.7
  160.5 73.9 %attend.3 = bf16[4608,128]{1,0:T(8,128)(2,1)S(1)} custom-call(bf16[4608,128]{1,0:T(8,128)(2,1)S(1)} %bitcast.21, bf16[4,768,768]{2,1,0:T(8,128)(2,1)S(1)} %copy-done.3, bf16[768,12]{1,0:T(8,128)(2,1)S(1)} %copy-done.5, bf16[128,512]{1,0:T(8,128)(2,1)S(1)} %copy-done.7, f32[1,128]{1,0:T(1,128)S(1)} %bitcast.25), custom_call_target="tpu_custom_call" | custom-call | flops 10871635968 | bytes 4718592 | tf_op jit(solution)/shard_map/attend/pallas_call | solution.py:367
  234.5 0.0 all-to-all-done.2
  234.5 0.0 copy-start
  234.5 0.0 copy-start.1
  234.5 30.3 %all_to_all.25 = bf16[64,72,128]{2,1,0:T(8,128)(2,1)S(1)} all-to-all(bf16[64,72,128]{2,1,0:T(8,128)(2,1)S(1)} %bitcast.22), channel_id=1, replica_groups=mesh['dap'=64,'dp'=2] {'dap'}, dimensions={0} | all-to-all | bytes 2359296 | tf_op jit(solution)/shard_map/all_to_all | solution.py:400
  264.8 0.0 copy-done
  264.8 0.0 copy-done.1
  264.8 3.1 %finish.1 = bf16[9216,128]{1,0:T(8,128)(2,1)} custom-call(bf16[4608,128]{1,0:T(8,128)(2,1)S(1)} %bitcast.18, bf16[4608,128]{1,0:T(8,128)(2,1)S(1)} %bitcast.19, bf16[128,128]{1,0:T(8,128)(2,1)S(1)} %copy-done, f32[1,128]{1,0:T(1,128)S(1)} %bitcast.23), custom_call_target="tpu_custom_call" | custom-call | tf_op jit(solution)/shard_map/finish/pallas_call | solution.py:404
  (2 shorter events, 0.0 us)
Async XLA Ops:
  6.0 18.3 %all-to-all-start = ((bf16[8,48,768]{2,1,0:T(8,128)(2,1)}), bf16[8,48,768]{2,1,0:T(8,128)(2,1)S(1)}, u32[]{:S(2)}, u32[]{:S(2)}) async-start(bf16[8,48,768]{2,1,0:T(8,128)(2,1)} %bitcast.30), calls=%async_computation | async-start | bytes 1179648 | tf_op jit(solution)/shard_map/all_to_all | solution.py:130
  24.3 0.8 copy-start.9
  25.1 20.6 %collective-permute-start.2 = (bf16[384,768]{1,0:T(8,128)(2,1)}, bf16[384,768]{1,0:T(8,128)(2,1)S(1)}, u32[]{:S(2)}, u32[]{:S(2)}) collective-permute-start(bf16[384,768]{1,0:T(8,128)(2,1)} %get-tuple-element.21.refs_0_), channel_id=1, source_target_pairs={{0,12},{2,50},{4,0},{6,54},{8,4},{10,58},{12,8},{14,62},{16,28},{1... | collective-permute-start | bytes 1769480 | tf_op jit(solution)/shard_map/ppermute | solution.py:139
  28.1 17.6 %collective-permute-start.1 = (bf16[384,768]{1,0:T(8,128)(2,1)}, bf16[384,768]{1,0:T(8,128)(2,1)S(1)}, u32[]{:S(2)}, u32[]{:S(2)}) collective-permute-start(bf16[384,768]{1,0:T(8,128)(2,1)} %get-tuple-element.21.refs_0_), channel_id=1, source_target_pairs={{0,8},{2,34},{4,12},{6,38},{8,0},{10,42},{12,4},{14,46},{16,24},{1... | collective-permute-start | bytes 1769480 | tf_op jit(solution)/shard_map/ppermute | solution.py:139
  28.4 22.4 %collective-permute-start = (bf16[384,768]{1,0:T(8,128)(2,1)}, bf16[384,768]{1,0:T(8,128)(2,1)S(1)}, u32[]{:S(2)}, u32[]{:S(2)}) collective-permute-start(bf16[384,768]{1,0:T(8,128)(2,1)} %get-tuple-element.21.refs_0_), channel_id=1, source_target_pairs={{0,4},{2,18},{4,8},{6,22},{8,12},{10,26},{12,0},{14,30},{16,20},{1... | collective-permute-start | bytes 1769480 | tf_op jit(solution)/shard_map/ppermute | solution.py:139
  29.0 9.0 %copy-start.10 = (bf16[384,768]{1,0:T(8,128)(2,1)S(1)}, bf16[384,768]{1,0:T(8,128)(2,1)}, u32[]{:S(2)}) copy-start(bf16[384,768]{1,0:T(8,128)(2,1)} %get-tuple-element.21.refs_0_) | copy-start | bytes 1769476
  29.0 33.7 %all-to-all-start.1 = ((bf16[64,72,128]{2,1,0:T(8,128)(2,1)}), bf16[64,72,128]{2,1,0:T(8,128)(2,1)S(1)}, u32[]{:S(2)}, u32[]{:S(2)}) async-start(bf16[64,72,128]{2,1,0:T(8,128)(2,1)} %bitcast.28), calls=%async_computation.1 | async-start | bytes 2359296 | tf_op jit(solution)/shard_map/all_to_all | solution.py:359
  38.1 15.8 %collective-permute-start.3 = (bf16[384,768]{1,0:T(8,128)(2,1)S(1)}, bf16[384,768]{1,0:T(8,128)(2,1)S(1)}, u32[]{:S(2)}, u32[]{:S(2)}) collective-permute-start(bf16[384,768]{1,0:T(8,128)(2,1)S(1)} %copy-done.10), channel_id=1, source_target_pairs={{0,2},{2,0},{4,6},{6,4},{8,10},{10,8},{12,14},{14,12},{16,18},{18,... | collective-permute-start | bytes 1769480 | tf_op jit(solution)/shard_map/ppermute | solution.py:141
  45.7 10.5 %copy-start.11 = (bf16[384,768]{1,0:T(8,128)(2,1)}, bf16[384,768]{1,0:T(8,128)(2,1)S(1)}, u32[]{:S(2)}) copy-start(bf16[384,768]{1,0:T(8,128)(2,1)S(1)} %collective-permute-done.2.refs_3_) | copy-start | bytes 1769476
  45.8 8.1 %collective-permute-start.6 = (bf16[384,768]{1,0:T(8,128)(2,1)S(1)}, bf16[384,768]{1,0:T(8,128)(2,1)S(1)}, u32[]{:S(2)}, u32[]{:S(2)}) collective-permute-start(bf16[384,768]{1,0:T(8,128)(2,1)S(1)} %collective-permute-done.2.refs_3_), channel_id=1, source_target_pairs={{0,2},{2,0},{4,6},{6,4},{8,10},{10,8},{12,14},{14,12},{16,18},{18,... | collective-permute-start | bytes 1769480 | tf_op jit(solution)/shard_map/ppermute | solution.py:141
  45.8 10.5 %copy-start.12 = (bf16[384,768]{1,0:T(8,128)(2,1)}, bf16[384,768]{1,0:T(8,128)(2,1)S(1)}, u32[]{:S(2)}) copy-start(bf16[384,768]{1,0:T(8,128)(2,1)S(1)} %collective-permute-done.1.refs_2_) | copy-start | bytes 1769476
  45.8 8.1 %collective-permute-start.5 = (bf16[384,768]{1,0:T(8,128)(2,1)S(1)}, bf16[384,768]{1,0:T(8,128)(2,1)S(1)}, u32[]{:S(2)}, u32[]{:S(2)}) collective-permute-start(bf16[384,768]{1,0:T(8,128)(2,1)S(1)} %collective-permute-done.1.refs_2_), channel_id=1, source_target_pairs={{0,2},{2,0},{4,6},{6,4},{8,10},{10,8},{12,14},{14,12},{16,18},{18,... | collective-permute-start | bytes 1769480 | tf_op jit(solution)/shard_map/ppermute | solution.py:141
  50.8 5.5 %copy-start.13 = (bf16[384,768]{1,0:T(8,128)(2,1)}, bf16[384,768]{1,0:T(8,128)(2,1)S(1)}, u32[]{:S(2)}) copy-start(bf16[384,768]{1,0:T(8,128)(2,1)S(1)} %collective-permute-done.refs_1_) | copy-start | bytes 1769476
  50.8 4.6 %collective-permute-start.4 = (bf16[384,768]{1,0:T(8,128)(2,1)S(1)}, bf16[384,768]{1,0:T(8,128)(2,1)S(1)}, u32[]{:S(2)}, u32[]{:S(2)}) collective-permute-start(bf16[384,768]{1,0:T(8,128)(2,1)S(1)} %collective-permute-done.refs_1_), channel_id=1, source_target_pairs={{0,2},{2,0},{4,6},{6,4},{8,10},{10,8},{12,14},{14,12},{16,18},{18,... | collective-permute-start | bytes 1769480 | tf_op jit(solution)/shard_map/ppermute | solution.py:141
  53.8 1.6 copy-start.14
  53.8 1.6 copy-start.15
  53.8 1.6 copy-start.16
  55.5 0.8 copy-start.17
  62.8 5.8 %copy-start.4 = (bf16[768,12]{1,0:T(8,128)(2,1)S(1)}, bf16[768,12]{1,0:T(8,128)(2,1)}, u32[]{:S(2)}) copy-start(bf16[768,12]{1,0:T(8,128)(2,1)} %get-tuple-element.24.present_ref) | copy-start | bytes 55300
  62.8 5.8 %copy-start.6 = (bf16[128,512]{1,0:T(8,128)(2,1)S(1)}, bf16[128,512]{1,0:T(8,128)(2,1)}, u32[]{:S(2)}) copy-start(bf16[128,512]{1,0:T(8,128)(2,1)} %get-tuple-element.25.weight_ref) | copy-start | bytes 393220
  62.8 5.8 %copy-start.8 = (f32[128]{0:T(128)S(1)}, f32[128]{0:T(128)}, u32[]{:S(2)}) copy-start(f32[128]{0:T(128)} %param.21) | copy-start | bytes 1540
  62.8 83.1 %all-to-all-start.3 = ((bf16[64,72,128]{2,1,0:T(8,128)(2,1)}), bf16[64,72,128]{2,1,0:T(8,128)(2,1)S(1)}, u32[]{:S(2)}, u32[]{:S(2)}) async-start(bf16[64,72,128]{2,1,0:T(8,128)(2,1)} %bitcast.26), calls=%async_computation.3 | async-start | bytes 2359296 | tf_op jit(solution)/shard_map/all_to_all | solution.py:359
  68.6 2.3 copy-start.2
  146.0 88.5 %all-to-all-start.2 = ((bf16[64,72,128]{2,1,0:T(8,128)(2,1)}), bf16[64,72,128]{2,1,0:T(8,128)(2,1)S(1)}, u32[]{:S(2)}, u32[]{:S(2)}) async-start(bf16[64,72,128]{2,1,0:T(8,128)(2,1)} %bitcast.10), calls=%async_computation.2 | async-start | bytes 2359296 | tf_op jit(solution)/shard_map/all_to_all | solution.py:400
  156.4 2.3 copy-start.3
  158.7 0.9 copy-start.5
  159.6 0.9 copy-start.7
  234.5 30.3 %copy-start = (bf16[128,128]{1,0:T(8,128)(2,1)S(1)}, bf16[128,128]{1,0:T(8,128)(2,1)}, u32[]{:S(2)}) copy-start(bf16[128,128]{1,0:T(8,128)(2,1)} %refs_2_.3) | copy-start | bytes 98308
  234.5 30.3 %copy-start.1 = (f32[128]{0:T(128)S(1)}, f32[128]{0:T(128)}, u32[]{:S(2)}) copy-start(f32[128]{0:T(128)} %param.23) | copy-start | bytes 1540
where the time goes:
time: 269 us; the launch traced here: 268 us
  Pallas kernels  169 us (63%)
  starting transfers between devices  41.3 us (15%)
  blocking collectives  30.3 us (11%)
  waiting for transfers between devices  18.9 us (7%)
  local copies, waits for them, and re-layouts  8.16 us (3%)
    pallas_call x2, Pallas kernels, local(): pl.pallas_call(functools.partial(attend_kernel, chunk, per, heads), out_s...  149 us
    all_to_all x1, blocking collectives, local(): lax.all_to_all(gated.reshape(groups, rows * per, channels), 'dap', split_...  30.3 us
    all_to_all x2, starting transfers between devices, local(): lax.all_to_all(send.reshape(groups, rows * per, channels), 'dap', split_a...  14.8 us
    ppermute x3, waiting for transfers between devices, gather_bias(): lax.ppermute(first, 'dap', second_pairs(step))  11.7 us
    all_to_all x1, starting transfers between devices, local(): lax.all_to_all(gated.reshape(groups, rows * per, channels), 'dap', split_...  10.4 us
    unnamed x36, local copies, waits for them, and re-layouts  8.16 us
    all_to_all x1, starting transfers between devices, gather_bias(): lax.all_to_all(bias_copies.reshape((FIRST, bias_copies.shape[0] // FIRST,...  8.16 us
    pallas_call x1, Pallas kernels, local(): pl.pallas_call(functools.partial(turn_kernel, heads, rows, len(later)), o...  6.51 us
  transfers between devices with their start and end apart: 11, of which 4 were waited for; matrix products, arithmetic and copies ran while one was open for 0% of the time, Pallas kernels for 60%

commit v1 on v0

--- a/solution.py
+++ b/solution.py
@@ -11,6 +11,7 @@
 EPSILON = 1e-05
 CHUNKS = 2
 ATTEND_MIB = 40
+MASK_ROWS = 16
 TURN_MIB = 60
 FINISH_MIB = 30
 TOTAL_LOW = 1e-20
@@ -54,10 +55,8 @@
         bias_ref[pl.ds(copy * rows * heads, rows * heads), :] = wide_ref[...].astype(jnp.bfloat16)
 
 
-def layout_kernel(rows, width, groups, chunks, normed_ref, mask_ref, *refs):
-    weight_refs, chunk_refs = refs[:4], refs[4 : 4 + chunks]
-    present_ref, packed_ref, wide_ref = refs[4 + chunks : 7 + chunks]
-    staged_refs = refs[7 + chunks :]
+def layout_kernel(rows, width, groups, chunks, normed_ref, *refs):
+    chunk_refs, wide_ref, staged_refs = refs[:chunks], refs[chunks], refs[chunks + 1 :]
     cols = width // groups
     per = cols // chunks
     for row in range(rows):
@@ -69,10 +68,6 @@
             ]
     for chunk in range(chunks):
         chunk_refs[chunk][...] = staged_refs[chunk][...].astype(jnp.bfloat16)
-    present_ref[...] = mask_ref[...].astype(jnp.float32).T.astype(jnp.bfloat16)
-    channels = normed_ref.shape[1]
-    for at, ref in enumerate(weight_refs):
-        packed_ref[:, at * channels : (at + 1) * channels] = ref[...]
 
 
 def hold_kernel(*refs):
@@ -143,8 +138,9 @@
 
 def turn_kernel(heads, rows, handed, *refs):
     count = 2 * len(SHIFTS)
-    pieces, turned_ref, wide_ref = refs[:count], refs[count + handed], refs[-1]
-    width = turned_ref.shape[1]
+    pieces, mask_ref, weight_refs = refs[:count], refs[count], refs[count + 1 : count + 5]
+    held_ref, wide_ref = refs[count + 5 + handed], refs[-1]
+    width = held_ref.shape[1]
     tile = wide_ref.shape[2]
     here = place_of(lax.axis_index("dap"))
     block = rows * heads
@@ -174,7 +170,16 @@
     for head in range(heads):
         for at in range(0, width, tile):
             one = wide_ref[at // tile, pl.ds(head, width, stride=heads), :].astype(jnp.bfloat16)
-            turned_ref[head, pl.ds(at, tile), :] = dot_nt(unit, one).astype(jnp.bfloat16)
+            held_ref[pl.ds(head * width + at, tile), :] = dot_nt(unit, one).astype(jnp.bfloat16)
+    packed = jnp.concatenate([ref[...] for ref in weight_refs], axis=1)
+    weight_rows = packed.shape[0]
+    held_ref[pl.ds(heads * width, weight_rows), :] = jnp.concatenate(
+        [packed, jnp.zeros((weight_rows, width - packed.shape[1]), jnp.bfloat16)], axis=1
+    )
+    mask = mask_ref[...].astype(jnp.float32)
+    held_ref[pl.ds(heads * width + weight_rows, MASK_ROWS), :] = jnp.concatenate(
+        [mask, jnp.zeros((MASK_ROWS - mask.shape[0], width), jnp.float32)], axis=0
+    ).astype(jnp.bfloat16)
 
 
 def attend_kernel(
@@ -182,12 +187,11 @@
     per,
     heads,
     moved_ref,
-    bias_ref,
-    present_ref,
-    weight_ref,
+    held_ref,
     gate_offset_ref,
     out_ref,
     source_ref,
+    present_ref,
     result_ref,
     fine_ref,
     *sets,
@@ -196,6 +200,9 @@
     width, mask_cols = present_ref.shape
     head_dim = channels // heads
     source_ref[...] = moved_ref[...].astype(jnp.float32)
+    present_ref[...] = (
+        held_ref[pl.ds(heads * width + channels, mask_cols), :].astype(jnp.float32).T.astype(jnp.bfloat16)
+    )
     lane_head = lax.broadcasted_iota(jnp.int32, (1, channels), 1) // head_dim
     own = [(lane_head == head).astype(jnp.bfloat16) for head in range(heads)]
     fine_ref[...] = jnp.ones_like(fine_ref)
@@ -206,7 +213,7 @@
         query_ref, key_ref, value_ref, gate_ref, _ = buffers
         rows = pl.ds(part * share, share)
         source = source_ref[pl.ds(col + part * share * per, share, stride=per), :].astype(jnp.bfloat16)
-        wide = dot(source, weight_ref[...])
+        wide = dot(source, held_ref[pl.ds(heads * width, channels), : 4 * channels])
         query_ref[rows, :] = (wide[:, :channels] * head_dim ** (-0.5)).astype(jnp.bfloat16)
         key_ref[rows, :] = wide[:, channels : 2 * channels].astype(jnp.bfloat16)
         pick = (lax.broadcasted_iota(jnp.int32, (mask_cols, channels), 0) == chunk * per + col).astype(jnp.bfloat16)
@@ -218,7 +225,7 @@
 
     def attend(head, buffers):
         query_ref, key_ref, value_ref, _, total_ref = buffers
-        scores = dot_nt(query_ref[...] * own[head], key_ref[...]) + bias_ref[head].astype(jnp.float32)
+        scores = dot_nt(query_ref[...] * own[head], key_ref[...]) + held_ref[pl.ds(head * width, width), :].astype(jnp.float32)
         total = dot(jnp.exp(scores).astype(jnp.bfloat16), value_ref[...])
         for low in (head * head_dim, channels + head * head_dim):
             total_ref[:, low : low + head_dim] = total[:, low : low + head_dim]
@@ -261,7 +268,7 @@
                 for head in range(heads):
                     low = head * head_dim
                     scores = dot_nt(query_ref[rows, :] * own[head], key_ref[...])
-                    scores = scores + bias_ref[head, rows, :].astype(jnp.float32) + lift
+                    scores = scores + held_ref[pl.ds(pl.multiple_of(head * width + step * tile, tile), tile), :].astype(jnp.float32) + lift
                     probs = jnp.exp(scores - jnp.max(scores, axis=1, keepdims=True))
                     totals = jnp.sum(probs, axis=1, keepdims=True)
                     attended = dot(probs.astype(jnp.bfloat16), value_ref[:, :channels]) / totals
@@ -329,32 +336,31 @@
         compiler_params=params,
         name="norm",
     )(pair.reshape(rows * width, channels), ln_gain.reshape(1, channels), ln_offset.reshape(1, channels), bias_weight.T)
-    *sends, present, packed = pl.pallas_call(
+    sends = pl.pallas_call(
         functools.partial(layout_kernel, rows, width, groups, CHUNKS),
-        out_shape=[jax.ShapeDtypeStruct((block, channels), low)] * CHUNKS
-        + [jax.ShapeDtypeStruct((width, cols), low), jax.ShapeDtypeStruct((channels, 4 * channels), low)],
-        in_specs=in_vmem(6),
-        out_specs=in_vmem(CHUNKS + 2),
+        out_shape=[jax.ShapeDtypeStruct((block, channels), low)] * CHUNKS,
+        in_specs=in_vmem(1),
+        out_specs=in_vmem(CHUNKS),
         scratch_shapes=[pltpu.VMEM((2, width, channels), wide)] + [pltpu.VMEM((block, channels), wide)] * CHUNKS,
         compiler_params=params,
         cost_estimate=pl.CostEstimate(flops=10**6, bytes_accessed=15 * 10**6, transcendentals=0),
         name="layout",
-    )(normed, pair_mask.T, query_weight, key_weight, value_weight, gate_weight)
+    )(normed)
 
     pieces, sends = gather_bias(bias_copies, sends)
     whole = pl.BlockSpec(memory_space=pl.ANY)
     later = sends[1:]
-    turned, *later = pl.pallas_call(
+    held, *later = pl.pallas_call(
         functools.partial(turn_kernel, heads, rows, len(later)),
-        out_shape=[jax.ShapeDtypeStruct((heads, width, width), low)]
+        out_shape=[jax.ShapeDtypeStruct((heads * width + channels + MASK_ROWS, width), low)]
         + [jax.ShapeDtypeStruct(one.shape, one.dtype) for one in later],
-        in_specs=in_vmem(len(pieces)) + [whole] * len(later),
+        in_specs=in_vmem(len(pieces) + 5) + [whole] * len(later),
         out_specs=in_vmem(1) + [whole] * len(later),
-        input_output_aliases={len(pieces) + at: 1 + at for at in range(len(later))},
+        input_output_aliases={len(pieces) + 5 + at: 1 + at for at in range(len(later))},
         scratch_shapes=[pltpu.VMEM((width // channels, width * heads, channels), wide)],
         compiler_params=pltpu.CompilerParams(vmem_limit_bytes=TURN_MIB * 1024 * 1024),
         name="turn",
-    )(*pieces, *later)
+    )(*pieces, pair_mask.T, query_weight, key_weight, value_weight, gate_weight, *later)
     moved = [
         lax.all_to_all(
             send.reshape(groups, rows * per, channels), "dap", split_axis=0, concat_axis=0, tiled=True
@@ -367,10 +373,11 @@
         gated = pl.pallas_call(
             functools.partial(attend_kernel, chunk, per, heads),
             out_shape=jax.ShapeDtypeStruct((block, channels), low),
-            in_specs=in_vmem(5),
+            in_specs=in_vmem(3),
             out_specs=in_vmem(1)[0],
             scratch_shapes=[
                 pltpu.VMEM((block, channels), wide),
+                pltpu.VMEM((width, MASK_ROWS), low),
                 pltpu.VMEM((block, channels), wide),
                 pltpu.VMEM((8, channels), wide),
             ]
@@ -391,9 +398,7 @@
             name="attend",
         )(
             moved[chunk],
-            turned,
-            present,
-            packed,
+            held,
             gate_offset.reshape(1, channels),
         )
         returned.append(

time: 269 us -> 267 us (level)
    unnamed x36 -> x28, local copies, waits for them, and re-layouts: 8.16 us -> 6.47 us
where the time goes in v1:
time: 267 us; the launch traced here: 266 us
  Pallas kernels  169 us (63%)
  starting transfers between devices  41.2 us (15%)
  blocking collectives  30.3 us (11%)
  waiting for transfers between devices  19 us (7%)
  local copies, waits for them, and re-layouts  6.47 us (2%)
    pallas_call x2, Pallas kernels, local(): pl.pallas_call(functools.partial(attend_kernel, chunk, per, heads), out_s...  149 us
    all_to_all x1, blocking collectives, local(): lax.all_to_all(gated.reshape(groups, rows * per, channels), 'dap', split_...  30.3 us
    all_to_all x2, starting transfers between devices, local(): lax.all_to_all(send.reshape(groups, rows * per, channels), 'dap', split_a...  14.6 us
    ppermute x3, waiting for transfers between devices, gather_bias(): lax.ppermute(first, 'dap', second_pairs(step))  11.7 us
    all_to_all x1, starting transfers between devices, local(): lax.all_to_all(gated.reshape(groups, rows * per, channels), 'dap', split_...  10.4 us
    all_to_all x1, starting transfers between devices, gather_bias(): lax.all_to_all(bias_copies.reshape((FIRST, bias_copies.shape[0] // FIRST,...  8.16 us
    pallas_call x1, Pallas kernels, local(): pl.pallas_call(functools.partial(turn_kernel, heads, rows, len(later)), o...  6.62 us
    unnamed x28, local copies, waits for them, and re-layouts  6.47 us
  transfers between devices with their start and end apart: 11, of which 4 were waited for; matrix products, arithmetic and copies ran while one was open for 0% of the time, Pallas kernels for 60%

profile of v1, /device:TPU:1, one launch (start us, length us, event | category | flops | bytes accessed | tf_op | source)
XLA Modules:
  0.0 266.2 jit_solution(6102597486807731098)
XLA Ops:
  0.0 6.0 %norm.1 = (bf16[9216,128]{1,0:T(8,128)(2,1)}, bf16[384,768]{1,0:T(8,128)(2,1)}) custom-call(bf16[9216,128]{1,0:T(8,128)(2,1)} %bitcast.29, f32[1,128]{1,0:T(1,128)} %bitcast.33, f32[1,128]{1,0:T(1,128)} %bitcast.34, bf16[4,128]{1,0:T(4,128)(2,1)} %bitcast.32), custom_call_target="tpu_custom_call" | custom-call | tf_op jit(solution)/shard_map/norm/pallas_call | solution.py:327
  6.0 8.2 %all-to-all-start = ((bf16[8,48,768]{2,1,0:T(8,128)(2,1)}), bf16[8,48,768]{2,1,0:T(8,128)(2,1)S(1)}, u32[]{:S(2)}, u32[]{:S(2)}) async-start(bf16[8,48,768]{2,1,0:T(8,128)(2,1)} %bitcast.30), calls=%async_computation | async-start | bytes 1179648 | tf_op jit(solution)/shard_map/all_to_all | solution.py:125
  14.1 4.5 %layout.1 = (bf16[4608,128]{1,0:T(8,128)(2,1)}, bf16[4608,128]{1,0:T(8,128)(2,1)}) custom-call(bf16[9216,128]{1,0:T(8,128)(2,1)} %get-tuple-element.15.normed_ref), custom_call_target="tpu_custom_call" | custom-call | flops 1000000 | bytes 15000000 | tf_op jit(solution)/shard_map/layout/pallas_call | solution.py:339
  18.6 5.7 %all-to-all-done = bf16[8,48,768]{2,1,0:T(8,128)(2,1)S(1)} async-done(((bf16[8,48,768]{2,1,0:T(8,128)(2,1)}), bf16[8,48,768]{2,1,0:T(8,128)(2,1)S(1)}, u32[]{:S(2)}, u32[]{:S(2)}) %all-to-all-start) | async-done | bytes 589856 | tf_op jit(solution)/shard_map/all_to_all | solution.py:125
  24.3 0.0 copy-start.5
  24.3 0.8 copy-done.5
  25.1 3.0 %collective-permute-start.2 = (bf16[384,768]{1,0:T(8,128)(2,1)}, bf16[384,768]{1,0:T(8,128)(2,1)S(1)}, u32[]{:S(2)}, u32[]{:S(2)}) collective-permute-start(bf16[384,768]{1,0:T(8,128)(2,1)} %get-tuple-element.19.refs_0_), channel_id=1, source_target_pairs={{0,12},{2,50},{4,0},{6,54},{8,4},{10,58},{12,8},{14,62},{16,28},{1... | collective-permute-start | bytes 1769480 | tf_op jit(solution)/shard_map/ppermute | solution.py:134
  28.1 0.2 collective-permute-start.1
  28.4 0.7 collective-permute-start
  29.1 0.0 copy-start.6
  29.1 9.0 %all-to-all-start.1 = ((bf16[64,72,128]{2,1,0:T(8,128)(2,1)}), bf16[64,72,128]{2,1,0:T(8,128)(2,1)S(1)}, u32[]{:S(2)}, u32[]{:S(2)}) async-start(bf16[64,72,128]{2,1,0:T(8,128)(2,1)} %bitcast.28), calls=%async_computation.1 | async-start | bytes 2359296 | tf_op jit(solution)/shard_map/all_to_all | solution.py:365
  38.1 0.0 copy-done.6
  38.1 0.5 collective-permute-start.3
  38.6 7.2 %collective-permute-done.2.refs_3_ = bf16[384,768]{1,0:T(8,128)(2,1)S(1)} collective-permute-done((bf16[384,768]{1,0:T(8,128)(2,1)}, bf16[384,768]{1,0:T(8,128)(2,1)S(1)}, u32[]{:S(2)}, u32[]{:S(2)}) %collective-permute-start.2) | collective-permute-done | bytes 589856 | tf_op jit(solution)/shard_map/ppermute | solution.py:134
  45.8 0.0 copy-start.7
  45.8 0.0 collective-permute-start.6
  45.8 0.0 collective-permute-done.1.refs_2_
  45.8 0.0 copy-start.8
  45.8 0.5 collective-permute-start.5
  46.3 4.5 %collective-permute-done.refs_1_ = bf16[384,768]{1,0:T(8,128)(2,1)S(1)} collective-permute-done((bf16[384,768]{1,0:T(8,128)(2,1)}, bf16[384,768]{1,0:T(8,128)(2,1)S(1)}, u32[]{:S(2)}, u32[]{:S(2)}) %collective-permute-start) | collective-permute-done | bytes 589856 | tf_op jit(solution)/shard_map/ppermute | solution.py:134
  50.8 0.0 copy-start.9
  50.8 3.0 %collective-permute-start.4 = (bf16[384,768]{1,0:T(8,128)(2,1)S(1)}, bf16[384,768]{1,0:T(8,128)(2,1)S(1)}, u32[]{:S(2)}, u32[]{:S(2)}) collective-permute-start(bf16[384,768]{1,0:T(8,128)(2,1)S(1)} %collective-permute-done.refs_1_), channel_id=1, source_target_pairs={{0,2},{2,0},{4,6},{6,4},{8,10},{10,8},{12,14},{14,12},{16,18},{18,... | collective-permute-start | bytes 1769480 | tf_op jit(solution)/shard_map/ppermute | solution.py:136
  53.8 0.0 collective-permute-done.3.refs_4_
  53.8 0.0 copy-start.10
  53.8 0.0 collective-permute-done.6.refs_7_
  53.8 0.0 copy-start.11
  53.8 0.0 collective-permute-done.5.refs_6_
  53.9 0.0 copy-start.12
  53.9 1.6 collective-permute-done.4.refs_5_
  55.5 0.0 copy-done.10
  55.5 0.0 copy-start.13
  55.5 0.0 copy-done.11
  55.5 0.0 copy-done.12
  55.5 0.8 copy-done.13
  56.3 0.0 copy-done.7
  56.3 0.0 copy-done.8
  56.3 0.0 copy-done.9
  56.3 6.6 %turn.1 = (bf16[3216,768]{1,0:T(8,128)(2,1)}, bf16[4608,128]{1,0:T(8,128)(2,1)}) custom-call(bf16[384,768]{1,0:T(8,128)(2,1)} %get-tuple-element.19.refs_0_, bf16[384,768]{1,0:T(8,128)(2,1)} %copy-done.9, bf16[384,768]{1,0:T(8,128)(2,1)} %copy-done.8, bf16[384,768]{1,0:T(8,128)(2,1)} %copy-done.7, ...), custom_call_target="tpu_custom_call", output_to_operand_aliasing={{1}: (13, {})} | custom-call | tf_op jit(solution)/shard_map/turn/pallas_call | solution.py:353
  62.9 0.0 all-to-all-done.1
  62.9 0.0 copy-start.4
  62.9 5.7 %all-to-all-start.3 = ((bf16[64,72,128]{2,1,0:T(8,128)(2,1)}), bf16[64,72,128]{2,1,0:T(8,128)(2,1)S(1)}, u32[]{:S(2)}, u32[]{:S(2)}) async-start(bf16[64,72,128]{2,1,0:T(8,128)(2,1)} %bitcast.26), calls=%async_computation.3 | async-start | bytes 2359296 | tf_op jit(solution)/shard_map/all_to_all | solution.py:365
  68.6 0.0 copy-done.4
  68.6 0.0 copy-start.2
  68.6 2.4 copy-done.2
  71.0 75.0 %attend.2 = bf16[4608,128]{1,0:T(8,128)(2,1)} custom-call(bf16[4608,128]{1,0:T(8,128)(2,1)S(1)} %bitcast.20, bf16[3216,768]{1,0:T(8,128)(2,1)S(1)} %copy-done.2, f32[1,128]{1,0:T(1,128)S(1)} %bitcast.24), custom_call_target="tpu_custom_call" | custom-call | flops 10871635968 | bytes 4718592 | tf_op jit(solution)/shard_map/attend/pallas_call | solution.py:373
  146.0 0.0 all-to-all-done.3
  146.0 10.4 %all-to-all-start.2 = ((bf16[64,72,128]{2,1,0:T(8,128)(2,1)}), bf16[64,72,128]{2,1,0:T(8,128)(2,1)S(1)}, u32[]{:S(2)}, u32[]{:S(2)}) async-start(bf16[64,72,128]{2,1,0:T(8,128)(2,1)} %bitcast.10), calls=%async_computation.2 | async-start | bytes 2359296 | tf_op jit(solution)/shard_map/all_to_all | solution.py:405
  156.4 0.0 copy-start.3
  156.4 2.4 copy-done.3
  158.8 73.9 %attend.3 = bf16[4608,128]{1,0:T(8,128)(2,1)S(1)} custom-call(bf16[4608,128]{1,0:T(8,128)(2,1)S(1)} %bitcast.21, bf16[3216,768]{1,0:T(8,128)(2,1)S(1)} %copy-done.3, f32[1,128]{1,0:T(1,128)S(1)} %bitcast.25), custom_call_target="tpu_custom_call" | custom-call | flops 10871635968 | bytes 4718592 | tf_op jit(solution)/shard_map/attend/pallas_call | solution.py:373
  232.8 0.0 all-to-all-done.2
  232.8 0.0 copy-start
  232.8 0.0 copy-start.1
  232.8 30.3 %all_to_all.25 = bf16[64,72,128]{2,1,0:T(8,128)(2,1)S(1)} all-to-all(bf16[64,72,128]{2,1,0:T(8,128)(2,1)S(1)} %bitcast.22), channel_id=1, replica_groups=mesh['dap'=64,'dp'=2] {'dap'}, dimensions={0} | all-to-all | bytes 2359296 | tf_op jit(solution)/shard_map/all_to_all | solution.py:405
  263.1 0.0 copy-done
  263.1 0.0 copy-done.1
  263.1 3.1 %finish.1 = bf16[9216,128]{1,0:T(8,128)(2,1)} custom-call(bf16[4608,128]{1,0:T(8,128)(2,1)S(1)} %bitcast.18, bf16[4608,128]{1,0:T(8,128)(2,1)S(1)} %bitcast.19, bf16[128,128]{1,0:T(8,128)(2,1)S(1)} %copy-done, f32[1,128]{1,0:T(1,128)S(1)} %bitcast.23), custom_call_target="tpu_custom_call" | custom-call | tf_op jit(solution)/shard_map/finish/pallas_call | solution.py:409
  (1 shorter events, 0.0 us)
Async XLA Ops:
  6.0 18.3 %all-to-all-start = ((bf16[8,48,768]{2,1,0:T(8,128)(2,1)}), bf16[8,48,768]{2,1,0:T(8,128)(2,1)S(1)}, u32[]{:S(2)}, u32[]{:S(2)}) async-start(bf16[8,48,768]{2,1,0:T(8,128)(2,1)} %bitcast.30), calls=%async_computation | async-start | bytes 1179648 | tf_op jit(solution)/shard_map/all_to_all | solution.py:125
  24.3 0.8 copy-start.5
  25.1 20.6 %collective-permute-start.2 = (bf16[384,768]{1,0:T(8,128)(2,1)}, bf16[384,768]{1,0:T(8,128)(2,1)S(1)}, u32[]{:S(2)}, u32[]{:S(2)}) collective-permute-start(bf16[384,768]{1,0:T(8,128)(2,1)} %get-tuple-element.19.refs_0_), channel_id=1, source_target_pairs={{0,12},{2,50},{4,0},{6,54},{8,4},{10,58},{12,8},{14,62},{16,28},{1... | collective-permute-start | bytes 1769480 | tf_op jit(solution)/shard_map/ppermute | solution.py:134
  28.1 17.6 %collective-permute-start.1 = (bf16[384,768]{1,0:T(8,128)(2,1)}, bf16[384,768]{1,0:T(8,128)(2,1)S(1)}, u32[]{:S(2)}, u32[]{:S(2)}) collective-permute-start(bf16[384,768]{1,0:T(8,128)(2,1)} %get-tuple-element.19.refs_0_), channel_id=1, source_target_pairs={{0,8},{2,34},{4,12},{6,38},{8,0},{10,42},{12,4},{14,46},{16,24},{1... | collective-permute-start | bytes 1769480 | tf_op jit(solution)/shard_map/ppermute | solution.py:134
  28.4 22.4 %collective-permute-start = (bf16[384,768]{1,0:T(8,128)(2,1)}, bf16[384,768]{1,0:T(8,128)(2,1)S(1)}, u32[]{:S(2)}, u32[]{:S(2)}) collective-permute-start(bf16[384,768]{1,0:T(8,128)(2,1)} %get-tuple-element.19.refs_0_), channel_id=1, source_target_pairs={{0,4},{2,18},{4,8},{6,22},{8,12},{10,26},{12,0},{14,30},{16,20},{1... | collective-permute-start | bytes 1769480 | tf_op jit(solution)/shard_map/ppermute | solution.py:134
  29.1 9.0 %copy-start.6 = (bf16[384,768]{1,0:T(8,128)(2,1)S(1)}, bf16[384,768]{1,0:T(8,128)(2,1)}, u32[]{:S(2)}) copy-start(bf16[384,768]{1,0:T(8,128)(2,1)} %get-tuple-element.19.refs_0_) | copy-start | bytes 1769476
  29.1 33.9 %all-to-all-start.1 = ((bf16[64,72,128]{2,1,0:T(8,128)(2,1)}), bf16[64,72,128]{2,1,0:T(8,128)(2,1)S(1)}, u32[]{:S(2)}, u32[]{:S(2)}) async-start(bf16[64,72,128]{2,1,0:T(8,128)(2,1)} %bitcast.28), calls=%async_computation.1 | async-start | bytes 2359296 | tf_op jit(solution)/shard_map/all_to_all | solution.py:365
  38.1 15.8 %collective-permute-start.3 = (bf16[384,768]{1,0:T(8,128)(2,1)S(1)}, bf16[384,768]{1,0:T(8,128)(2,1)S(1)}, u32[]{:S(2)}, u32[]{:S(2)}) collective-permute-start(bf16[384,768]{1,0:T(8,128)(2,1)S(1)} %copy-done.6), channel_id=1, source_target_pairs={{0,2},{2,0},{4,6},{6,4},{8,10},{10,8},{12,14},{14,12},{16,18},{18,... | collective-permute-start | bytes 1769480 | tf_op jit(solution)/shard_map/ppermute | solution.py:136
  45.8 10.5 %copy-start.7 = (bf16[384,768]{1,0:T(8,128)(2,1)}, bf16[384,768]{1,0:T(8,128)(2,1)S(1)}, u32[]{:S(2)}) copy-start(bf16[384,768]{1,0:T(8,128)(2,1)S(1)} %collective-permute-done.2.refs_3_) | copy-start | bytes 1769476
  45.8 8.1 %collective-permute-start.6 = (bf16[384,768]{1,0:T(8,128)(2,1)S(1)}, bf16[384,768]{1,0:T(8,128)(2,1)S(1)}, u32[]{:S(2)}, u32[]{:S(2)}) collective-permute-start(bf16[384,768]{1,0:T(8,128)(2,1)S(1)} %collective-permute-done.2.refs_3_), channel_id=1, source_target_pairs={{0,2},{2,0},{4,6},{6,4},{8,10},{10,8},{12,14},{14,12},{16,18},{18,... | collective-permute-start | bytes 1769480 | tf_op jit(solution)/shard_map/ppermute | solution.py:136
  45.8 10.5 %copy-start.8 = (bf16[384,768]{1,0:T(8,128)(2,1)}, bf16[384,768]{1,0:T(8,128)(2,1)S(1)}, u32[]{:S(2)}) copy-start(bf16[384,768]{1,0:T(8,128)(2,1)S(1)} %collective-permute-done.1.refs_2_) | copy-start | bytes 1769476
  45.8 8.1 %collective-permute-start.5 = (bf16[384,768]{1,0:T(8,128)(2,1)S(1)}, bf16[384,768]{1,0:T(8,128)(2,1)S(1)}, u32[]{:S(2)}, u32[]{:S(2)}) collective-permute-start(bf16[384,768]{1,0:T(8,128)(2,1)S(1)} %collective-permute-done.1.refs_2_), channel_id=1, source_target_pairs={{0,2},{2,0},{4,6},{6,4},{8,10},{10,8},{12,14},{14,12},{16,18},{18,... | collective-permute-start | bytes 1769480 | tf_op jit(solution)/shard_map/ppermute | solution.py:136
  50.8 5.5 %copy-start.9 = (bf16[384,768]{1,0:T(8,128)(2,1)}, bf16[384,768]{1,0:T(8,128)(2,1)S(1)}, u32[]{:S(2)}) copy-start(bf16[384,768]{1,0:T(8,128)(2,1)S(1)} %collective-permute-done.refs_1_) | copy-start | bytes 1769476
  50.8 4.6 %collective-permute-start.4 = (bf16[384,768]{1,0:T(8,128)(2,1)S(1)}, bf16[384,768]{1,0:T(8,128)(2,1)S(1)}, u32[]{:S(2)}, u32[]{:S(2)}) collective-permute-start(bf16[384,768]{1,0:T(8,128)(2,1)S(1)} %collective-permute-done.refs_1_), channel_id=1, source_target_pairs={{0,2},{2,0},{4,6},{6,4},{8,10},{10,8},{12,14},{14,12},{16,18},{18,... | collective-permute-start | bytes 1769480 | tf_op jit(solution)/shard_map/ppermute | solution.py:136
  53.8 1.6 copy-start.10
  53.8 1.6 copy-start.11
  53.9 1.6 copy-start.12
  55.5 0.8 copy-start.13
  62.9 5.7 %copy-start.4 = (f32[128]{0:T(128)S(1)}, f32[128]{0:T(128)}, u32[]{:S(2)}) copy-start(f32[128]{0:T(128)} %param.21) | copy-start | bytes 1540
  62.9 83.1 %all-to-all-start.3 = ((bf16[64,72,128]{2,1,0:T(8,128)(2,1)}), bf16[64,72,128]{2,1,0:T(8,128)(2,1)S(1)}, u32[]{:S(2)}, u32[]{:S(2)}) async-start(bf16[64,72,128]{2,1,0:T(8,128)(2,1)} %bitcast.26), calls=%async_computation.3 | async-start | bytes 2359296 | tf_op jit(solution)/shard_map/all_to_all | solution.py:365
  68.6 2.4 copy-start.2
  146.0 86.8 %all-to-all-start.2 = ((bf16[64,72,128]{2,1,0:T(8,128)(2,1)}), bf16[64,72,128]{2,1,0:T(8,128)(2,1)S(1)}, u32[]{:S(2)}, u32[]{:S(2)}) async-start(bf16[64,72,128]{2,1,0:T(8,128)(2,1)} %bitcast.10), calls=%async_computation.2 | async-start | bytes 2359296 | tf_op jit(solution)/shard_map/all_to_all | solution.py:405
  156.4 2.4 copy-start.3
  232.8 30.3 %copy-start = (bf16[128,128]{1,0:T(8,128)(2,1)S(1)}, bf16[128,128]{1,0:T(8,128)(2,1)}, u32[]{:S(2)}) copy-start(bf16[128,128]{1,0:T(8,128)(2,1)} %refs_2_.1) | copy-start | bytes 98308
  232.8 30.3 %copy-start.1 = (f32[128]{0:T(128)S(1)}, f32[128]{0:T(128)}, u32[]{:S(2)}) copy-start(f32[128]{0:T(128)} %param.23) | copy-start | bytes 1540

commit v2 on v1

--- a/solution.py
+++ b/solution.py
@@ -12,7 +12,8 @@
 CHUNKS = 2
 ATTEND_MIB = 40
 MASK_ROWS = 16
-TURN_MIB = 60
+TURN_MIB = 30
+ROOM = 8
 FINISH_MIB = 30
 TOTAL_LOW = 1e-20
 TOTAL_HIGH = 1e30
@@ -36,31 +37,46 @@
     return [pl.BlockSpec(memory_space=pltpu.VMEM)] * count
 
 
-def norm_kernel(rows, width, heads, pair_ref, gain_ref, offset_ref, bias_weight_ref, normed_ref, bias_ref, wide_ref):
+def normalise(block, gain_ref, offset_ref):
+    wide = block.astype(jnp.float32)
+    centred = wide - jnp.mean(wide, axis=1, keepdims=True)
+    spread = jnp.mean(centred * centred, axis=1, keepdims=True)
+    return (centred * lax.rsqrt(spread + EPSILON) * gain_ref[...] + offset_ref[...]).astype(jnp.bfloat16)
+
+
+def norm_kernel(rows, width, heads, pair_ref, gain_ref, offset_ref, bias_weight_ref, bias_ref, wide_ref):
     weight = bias_weight_ref[...]
     blank = jnp.zeros_like(weight)
     both = jnp.concatenate(
         [jnp.concatenate([weight, blank], axis=1), jnp.concatenate([blank, weight], axis=1)], axis=0
     )
-    for row in range(rows):
-        wide = pair_ref[pl.ds(row * width, width), :].astype(jnp.float32)
-        centred = wide - jnp.mean(wide, axis=1, keepdims=True)
-        spread = jnp.mean(centred * centred, axis=1, keepdims=True)
-        normed = centred * lax.rsqrt(spread + EPSILON) * gain_ref[...] + offset_ref[...]
-        normed_ref[pl.ds(row * width, width), :] = normed.astype(jnp.bfloat16)
-        if row % 2:
-            two = [normed_ref[pl.ds(at * width, width), :] for at in (row - 1, row)]
-            wide_ref[pl.ds((row - 1) * heads, 2 * heads), :] = dot_nt(both, jnp.concatenate(two, axis=1))
+    for row in range(0, rows, 2):
+        two = [normalise(pair_ref[pl.ds(at * width, width), :], gain_ref, offset_ref) for at in (row, row + 1)]
+        wide_ref[pl.ds(row * heads, 2 * heads), :] = dot_nt(both, jnp.concatenate(two, axis=1))
     for copy in range(bias_ref.shape[0] // (rows * heads)):
         bias_ref[pl.ds(copy * rows * heads, rows * heads), :] = wide_ref[...].astype(jnp.bfloat16)
 
 
-def layout_kernel(rows, width, groups, chunks, normed_ref, *refs):
-    chunk_refs, wide_ref, staged_refs = refs[:chunks], refs[chunks], refs[chunks + 1 :]
+def layout_kernel(rows, width, groups, chunks, start, pair_ref, gain_ref, offset_ref, _, mask_ref, *refs):
+    weight_refs, chunk_refs, whole_ref = refs[:4], refs[4 : 4 + chunks], refs[4 + chunks]
+    tail_ref, sem, wide_ref = refs[5 + chunks : 8 + chunks]
+    staged_refs = refs[8 + chunks :]
+    packed = jnp.concatenate([ref[...] for ref in weight_refs], axis=1)
+    weight_rows = packed.shape[0]
+    tail_ref[pl.ds(0, weight_rows), :] = jnp.concatenate(
+        [packed, jnp.zeros((weight_rows, width - packed.shape[1]), jnp.bfloat16)], axis=1
+    )
+    mask = mask_ref[...].astype(jnp.float32)
+    tail_ref[pl.ds(weight_rows, MASK_ROWS), :] = jnp.concatenate(
+        [mask, jnp.zeros((MASK_ROWS - mask.shape[0], width), jnp.float32)], axis=0
+    ).astype(jnp.bfloat16)
+    store = pltpu.make_async_copy(tail_ref, whole_ref.at[pl.ds(start, weight_rows + MASK_ROWS), :], sem)
+    store.start()
     cols = width // groups
     per = cols // chunks
     for row in range(rows):
-        wide_ref[row % 2] = normed_ref[pl.ds(row * width, width), :].astype(jnp.float32)
+        normed = normalise(pair_ref[pl.ds(row * width, width), :], gain_ref, offset_ref)
+        wide_ref[row % 2] = normed.astype(jnp.float32)
         for col in range(cols):
             chunk, place = divmod(col, per)
             staged_refs[chunk][pl.ds(row * per + place, groups, stride=rows * per), :] = wide_ref[
@@ -68,6 +84,7 @@
             ]
     for chunk in range(chunks):
         chunk_refs[chunk][...] = staged_refs[chunk][...].astype(jnp.bfloat16)
+    store.wait()
 
 
 def hold_kernel(*refs):
@@ -138,8 +155,7 @@
 
 def turn_kernel(heads, rows, handed, *refs):
     count = 2 * len(SHIFTS)
-    pieces, mask_ref, weight_refs = refs[:count], refs[count], refs[count + 1 : count + 5]
-    held_ref, wide_ref = refs[count + 5 + handed], refs[-1]
+    pieces, whole_ref, (held_ref, wide_ref, sems) = refs[:count], refs[count + 1 + handed], refs[-3:]
     width = held_ref.shape[1]
     tile = wide_ref.shape[2]
     here = place_of(lax.axis_index("dap"))
@@ -167,19 +183,19 @@
     unit = (
         lax.broadcasted_iota(jnp.int32, (tile, tile), 0) == lax.broadcasted_iota(jnp.int32, (tile, tile), 1)
     ).astype(jnp.bfloat16)
+    stores = []
+
+    def store(at, rows_of):
+        stores.append(pltpu.make_async_copy(held_ref.at[rows_of, :], whole_ref.at[rows_of, :], sems.at[at]))
+        stores[at].start()
+
     for head in range(heads):
         for at in range(0, width, tile):
             one = wide_ref[at // tile, pl.ds(head, width, stride=heads), :].astype(jnp.bfloat16)
             held_ref[pl.ds(head * width + at, tile), :] = dot_nt(unit, one).astype(jnp.bfloat16)
-    packed = jnp.concatenate([ref[...] for ref in weight_refs], axis=1)
-    weight_rows = packed.shape[0]
-    held_ref[pl.ds(heads * width, weight_rows), :] = jnp.concatenate(
-        [packed, jnp.zeros((weight_rows, width - packed.shape[1]), jnp.bfloat16)], axis=1
-    )
-    mask = mask_ref[...].astype(jnp.float32)
-    held_ref[pl.ds(heads * width + weight_rows, MASK_ROWS), :] = jnp.concatenate(
-        [mask, jnp.zeros((MASK_ROWS - mask.shape[0], width), jnp.float32)], axis=0
-    ).astype(jnp.bfloat16)
+        store(head, pl.ds(head * width, width))
+    for one in stores:
+        one.wait()
 
 
 def attend_kernel(
@@ -324,43 +340,52 @@
     block = groups * rows * per
     low, wide = jnp.bfloat16, jnp.float32
     params = pltpu.CompilerParams(vmem_limit_bytes=60 * 1024 * 1024)
-    normed, bias_copies = pl.pallas_call(
+    flat = (pair.reshape(rows * width, channels), ln_gain.reshape(1, channels), ln_offset.reshape(1, channels))
+    bias_copies = pl.pallas_call(
         functools.partial(norm_kernel, rows, width, heads),
-        out_shape=[
-            jax.ShapeDtypeStruct((rows * width, channels), low),
-            jax.ShapeDtypeStruct((FIRST * rows * heads, width), low),
-        ],
+        out_shape=jax.ShapeDtypeStruct((FIRST * rows * heads, width), low),
         in_specs=in_vmem(4),
-        out_specs=in_vmem(2),
+        out_specs=in_vmem(1)[0],
         scratch_shapes=[pltpu.VMEM((rows * heads, width), wide)],
         compiler_params=params,
         name="norm",
-    )(pair.reshape(rows * width, channels), ln_gain.reshape(1, channels), ln_offset.reshape(1, channels), bias_weight.T)
-    sends = pl.pallas_call(
-        functools.partial(layout_kernel, rows, width, groups, CHUNKS),
-        out_shape=[jax.ShapeDtypeStruct((block, channels), low)] * CHUNKS,
-        in_specs=in_vmem(1),
-        out_specs=in_vmem(CHUNKS),
-        scratch_shapes=[pltpu.VMEM((2, width, channels), wide)] + [pltpu.VMEM((block, channels), wide)] * CHUNKS,
+    )(*flat, bias_weight.T)
+    whole = pl.BlockSpec(memory_space=pl.ANY)
+    tail_rows = channels + MASK_ROWS
+    held_rows = heads * width + tail_rows
+    *sends, held = pl.pallas_call(
+        functools.partial(layout_kernel, rows, width, groups, CHUNKS, heads * width),
+        out_shape=[jax.ShapeDtypeStruct((block, channels), low)] * CHUNKS
+        + [jax.ShapeDtypeStruct((ROOM * held_rows, width), low)],
+        in_specs=in_vmem(3) + [whole] + in_vmem(5),
+        out_specs=in_vmem(CHUNKS) + [whole],
+        scratch_shapes=[
+            pltpu.VMEM((tail_rows, width), low),
+            pltpu.SemaphoreType.DMA,
+            pltpu.VMEM((2, width, channels), wide),
+        ]
+        + [pltpu.VMEM((block, channels), wide)] * CHUNKS,
         compiler_params=params,
         cost_estimate=pl.CostEstimate(flops=10**6, bytes_accessed=15 * 10**6, transcendentals=0),
         name="layout",
-    )(normed)
+    )(*flat, bias_copies, pair_mask.T, query_weight, key_weight, value_weight, gate_weight)
 
     pieces, sends = gather_bias(bias_copies, sends)
-    whole = pl.BlockSpec(memory_space=pl.ANY)
     later = sends[1:]
     held, *later = pl.pallas_call(
         functools.partial(turn_kernel, heads, rows, len(later)),
-        out_shape=[jax.ShapeDtypeStruct((heads * width + channels + MASK_ROWS, width), low)]
-        + [jax.ShapeDtypeStruct(one.shape, one.dtype) for one in later],
-        in_specs=in_vmem(len(pieces) + 5) + [whole] * len(later),
-        out_specs=in_vmem(1) + [whole] * len(later),
-        input_output_aliases={len(pieces) + 5 + at: 1 + at for at in range(len(later))},
-        scratch_shapes=[pltpu.VMEM((width // channels, width * heads, channels), wide)],
+        out_shape=[jax.ShapeDtypeStruct(one.shape, one.dtype) for one in (held, *later)],
+        in_specs=in_vmem(len(pieces)) + [whole] * (1 + len(later)),
+        out_specs=[whole] * (1 + len(later)),
+        input_output_aliases={len(pieces) + at: at for at in range(1 + len(later))},
+        scratch_shapes=[
+            pltpu.VMEM((heads * width, width), low),
+            pltpu.VMEM((width // channels, width * heads, channels), wide),
+            pltpu.SemaphoreType.DMA((heads,)),
+        ],
         compiler_params=pltpu.CompilerParams(vmem_limit_bytes=TURN_MIB * 1024 * 1024),
         name="turn",
-    )(*pieces, pair_mask.T, query_weight, key_weight, value_weight, gate_weight, *later)
+    )(*pieces, held, *later)
     moved = [
         lax.all_to_all(
             send.reshape(groups, rows * per, channels), "dap", split_axis=0, concat_axis=0, tiled=True
@@ -373,7 +398,10 @@
         gated = pl.pallas_call(
             functools.partial(attend_kernel, chunk, per, heads),
             out_shape=jax.ShapeDtypeStruct((block, channels), low),
-            in_specs=in_vmem(3),
+            grid=(1,),
+            in_specs=in_vmem(1)
+            + [pl.BlockSpec((held_rows, width), lambda step: (0, 0), pipeline_mode=pl.Buffered(1))]
+            + in_vmem(1),
             out_specs=in_vmem(1)[0],
             scratch_shapes=[
                 pltpu.VMEM((block, channels), wide),

time: 267 us -> 265 us (level)
  local copies, waits for them, and re-layouts: 6.47 us -> 0.85 us
  Pallas kernels: 169 us -> 173 us
    unnamed x28 -> x10, local copies, waits for them, and re-layouts: 6.47 us -> 0.85 us
    pallas_call x2, Pallas kernels: 149 us -> 154 us  [local(): pl.pallas_call(functools.partial(attend_kernel, chunk, per, heads), out_s...]
    pallas_call x1, Pallas kernels: 6.62 us -> 3.31 us  [local(): pl.pallas_call(functools.partial(turn_kernel, heads, rows, len(later)), o...]
    all_to_all x1, waiting for transfers between devices: 5.71 us -> 2.93 us  [gather_bias(): lax.all_to_all(bias_copies.reshape((FIRST, bias_copies.shape[0] // FIRST,...]
    pallas_call x1, Pallas kernels: 4.48 us -> 7.25 us  [local(): pl.pallas_call(functools.partial(layout_kernel, rows, width, groups, CHUN...]
  transfers between devices with their start and end apart: 11 -> 11, of which waited for: 4 -> 5; matrix products, arithmetic and copies ran while one was open for 0% -> 0% of each run, Pallas kernels for 60% -> 62%
where the time goes in v2:
time: 265 us
  Pallas kernels  173 us (65%)
  starting transfers between devices  42.2 us (16%)
  blocking collectives  30.3 us (11%)
  waiting for transfers between devices  18.5 us (7%)
    pallas_call x2, Pallas kernels, local(): pl.pallas_call(functools.partial(attend_kernel, chunk, per, heads), out_s...  154 us
    all_to_all x1, blocking collectives, local(): lax.all_to_all(gated.reshape(groups, rows * per, channels), 'dap', split_...  30.3 us
    all_to_all x2, starting transfers between devices, local(): lax.all_to_all(send.reshape(groups, rows * per, channels), 'dap', split_a...  15.7 us
    ppermute x3, waiting for transfers between devices, gather_bias(): lax.ppermute(first, 'dap', second_pairs(step))  11.7 us
    all_to_all x1, starting transfers between devices, local(): lax.all_to_all(gated.reshape(groups, rows * per, channels), 'dap', split_...  10.4 us
    all_to_all x1, starting transfers between devices, gather_bias(): lax.all_to_all(bias_copies.reshape((FIRST, bias_copies.shape[0] // FIRST,...  8.16 us
    pallas_call x1, Pallas kernels, local(): pl.pallas_call(functools.partial(layout_kernel, rows, width, groups, CHUN...  7.25 us
  transfers between devices with their start and end apart: 11, of which 5 were waited for; matrix products, arithmetic and copies ran while one was open for 0% of the time, Pallas kernels for 62%

profile of v2, /device:TPU:1, one launch (start us, length us, event | category | flops | bytes accessed | tf_op | source)
XLA Modules:
  0.0 264.8 jit_solution(15566953509240764781)
XLA Ops:
  0.0 5.2 %norm.1._ = bf16[384,768]{1,0:T(8,128)(2,1)} custom-call(bf16[9216,128]{1,0:T(8,128)(2,1)} %bitcast.27, f32[1,128]{1,0:T(1,128)} %bitcast.32, f32[1,128]{1,0:T(1,128)} %bitcast.34, bf16[4,128]{1,0:T(4,128)(2,1)} %bitcast.36), custom_call_target="tpu_custom_call" | custom-call | tf_op jit(solution)/shard_map/norm/pallas_call | solution.py:344
  5.2 8.2 %all-to-all-start = ((bf16[8,48,768]{2,1,0:T(8,128)(2,1)}), bf16[8,48,768]{2,1,0:T(8,128)(2,1)S(1)}, u32[]{:S(2)}, u32[]{:S(2)}) async-start(bf16[8,48,768]{2,1,0:T(8,128)(2,1)} %bitcast.29), calls=%async_computation | async-start | bytes 1179648 | tf_op jit(solution)/shard_map/all_to_all | solution.py:142
  13.4 7.2 %layout.1 = (bf16[4608,128]{1,0:T(8,128)(2,1)}, bf16[4608,128]{1,0:T(8,128)(2,1)}, bf16[25728,768]{1,0:T(8,128)(2,1)}) custom-call(bf16[9216,128]{1,0:T(8,128)(2,1)} %bitcast.28, f32[1,128]{1,0:T(1,128)} %bitcast.33, f32[1,128]{1,0:T(1,128)} %bitcast.35, bf16[384,768]{1,0:T(8,128)(2,1)} %norm.1._, s32[12,768]{1,0:T(8,128)} %bitcast.31, ...), custom_call_target="tpu_custom_call" | custom-call | flops 1000000 | bytes 15000000 | tf_op jit(solution)/shard_map/layout/pallas_call | solution.py:356
  20.6 2.9 %all-to-all-done = bf16[8,48,768]{2,1,0:T(8,128)(2,1)S(1)} async-done(((bf16[8,48,768]{2,1,0:T(8,128)(2,1)}), bf16[8,48,768]{2,1,0:T(8,128)(2,1)S(1)}, u32[]{:S(2)}, u32[]{:S(2)}) %all-to-all-start) | async-done | bytes 589856 | tf_op jit(solution)/shard_map/all_to_all | solution.py:142
  23.6 0.0 copy-start
  23.6 0.8 copy-done
  24.4 3.0 %collective-permute-start.2 = (bf16[384,768]{1,0:T(8,128)(2,1)}, bf16[384,768]{1,0:T(8,128)(2,1)S(1)}, u32[]{:S(2)}, u32[]{:S(2)}) collective-permute-start(bf16[384,768]{1,0:T(8,128)(2,1)} %get-tuple-element.16.refs_0_), channel_id=1, source_target_pairs={{0,12},{2,50},{4,0},{6,54},{8,4},{10,58},{12,8},{14,62},{16,28},{1... | collective-permute-start | bytes 1769480 | tf_op jit(solution)/shard_map/ppermute | solution.py:151
  27.4 0.2 collective-permute-start.1
  27.6 0.7 collective-permute-start
  28.3 0.0 copy-start.1
  28.3 9.0 %all-to-all-start.1 = ((bf16[64,72,128]{2,1,0:T(8,128)(2,1)}), bf16[64,72,128]{2,1,0:T(8,128)(2,1)S(1)}, u32[]{:S(2)}, u32[]{:S(2)}) async-start(bf16[64,72,128]{2,1,0:T(8,128)(2,1)} %bitcast.30), calls=%async_computation.1 | async-start | bytes 2359296 | tf_op jit(solution)/shard_map/all_to_all | solution.py:390
  37.3 0.0 copy-done.1
  37.3 0.5 collective-permute-start.3
  37.9 7.2 %collective-permute-done.2.refs_3_ = bf16[384,768]{1,0:T(8,128)(2,1)S(1)} collective-permute-done((bf16[384,768]{1,0:T(8,128)(2,1)}, bf16[384,768]{1,0:T(8,128)(2,1)S(1)}, u32[]{:S(2)}, u32[]{:S(2)}) %collective-permute-start.2) | collective-permute-done | bytes 589856 | tf_op jit(solution)/shard_map/ppermute | solution.py:151
  45.0 0.0 collective-permute-start.6
  45.0 0.0 collective-permute-done.1.refs_2_
  45.0 0.5 collective-permute-start.5
  45.5 4.5 %collective-permute-done.refs_1_ = bf16[384,768]{1,0:T(8,128)(2,1)S(1)} collective-permute-done((bf16[384,768]{1,0:T(8,128)(2,1)}, bf16[384,768]{1,0:T(8,128)(2,1)S(1)}, u32[]{:S(2)}, u32[]{:S(2)}) %collective-permute-start) | collective-permute-done | bytes 589856 | tf_op jit(solution)/shard_map/ppermute | solution.py:151
  50.1 3.0 %collective-permute-start.4 = (bf16[384,768]{1,0:T(8,128)(2,1)S(1)}, bf16[384,768]{1,0:T(8,128)(2,1)S(1)}, u32[]{:S(2)}, u32[]{:S(2)}) collective-permute-start(bf16[384,768]{1,0:T(8,128)(2,1)S(1)} %collective-permute-done.refs_1_), channel_id=1, source_target_pairs={{0,2},{2,0},{4,6},{6,4},{8,10},{10,8},{12,14},{14,12},{16,18},{18,... | collective-permute-start | bytes 1769480 | tf_op jit(solution)/shard_map/ppermute | solution.py:153
  53.1 0.0 collective-permute-done.3.refs_4_
  53.1 0.0 collective-permute-done.6.refs_7_
  53.1 0.0 collective-permute-done.5.refs_6_
  53.1 1.6 collective-permute-done.4.refs_5_
  54.7 3.3 %turn.1 = (bf16[25728,768]{1,0:T(8,128)(2,1)}, bf16[4608,128]{1,0:T(8,128)(2,1)}) custom-call(bf16[384,768]{1,0:T(8,128)(2,1)S(1)} %copy-done.1, bf16[384,768]{1,0:T(8,128)(2,1)S(1)} %collective-permute-done.refs_1_, bf16[384,768]{1,0:T(8,128)(2,1)S(1)} %collective-permute-done.1.refs_2_, ...), custom_call_target="tpu_custom_call", output_to_operand_aliasing={{0}: (8, {}), {1}: (9, {})} | custom-call | tf_op jit(solution)/shard_map/turn/pallas_call | solution.py:375
  58.0 2.2 all-to-all-done.1
  60.2 0.0 copy-start.3
  60.2 6.7 %all-to-all-start.3 = ((bf16[64,72,128]{2,1,0:T(8,128)(2,1)}), bf16[64,72,128]{2,1,0:T(8,128)(2,1)S(1)}, u32[]{:S(2)}, u32[]{:S(2)}) async-start(bf16[64,72,128]{2,1,0:T(8,128)(2,1)} %bitcast.12), calls=%async_computation.3 | async-start | bytes 2359296 | tf_op jit(solution)/shard_map/all_to_all | solution.py:390
  66.9 0.0 copy-done.3
  66.9 77.5 %attend.2 = bf16[4608,128]{1,0:T(8,128)(2,1)} custom-call(bf16[4608,128]{1,0:T(8,128)(2,1)S(1)} %bitcast.19, bf16[25728,768]{1,0:T(8,128)(2,1)} %get-tuple-element.19.held_ref, f32[1,128]{1,0:T(1,128)S(1)} %bitcast.24), custom_call_target="tpu_custom_call" | custom-call | flops 10871635968 | bytes 4718592 | tf_op jit(solution)/shard_map/attend/pallas_call | solution.py:398
  144.4 0.0 all-to-all-done.3
  144.4 10.4 %all-to-all-start.2 = ((bf16[64,72,128]{2,1,0:T(8,128)(2,1)}), bf16[64,72,128]{2,1,0:T(8,128)(2,1)S(1)}, u32[]{:S(2)}, u32[]{:S(2)}) async-start(bf16[64,72,128]{2,1,0:T(8,128)(2,1)} %bitcast.10), calls=%async_computation.2 | async-start | bytes 2359296 | tf_op jit(solution)/shard_map/all_to_all | solution.py:433
  154.8 76.5 %attend.3 = bf16[4608,128]{1,0:T(8,128)(2,1)S(1)} custom-call(bf16[4608,128]{1,0:T(8,128)(2,1)S(1)} %bitcast.20, bf16[25728,768]{1,0:T(8,128)(2,1)} %get-tuple-element.19.held_ref, f32[1,128]{1,0:T(1,128)S(1)} %bitcast.25), custom_call_target="tpu_custom_call" | custom-call | flops 10871635968 | bytes 4718592 | tf_op jit(solution)/shard_map/attend/pallas_call | solution.py:398
  231.3 0.0 all-to-all-done.2
  231.3 0.0 copy-start.2
  231.3 0.0 copy-start.4
  231.4 30.3 %all_to_all.25 = bf16[64,72,128]{2,1,0:T(8,128)(2,1)S(1)} all-to-all(bf16[64,72,128]{2,1,0:T(8,128)(2,1)S(1)} %bitcast.21), channel_id=1, replica_groups=mesh['dap'=64,'dp'=2] {'dap'}, dimensions={0} | all-to-all | bytes 2359296 | tf_op jit(solution)/shard_map/all_to_all | solution.py:433
  261.7 0.0 copy-done.2
  261.7 0.0 copy-done.4
  261.7 3.1 %finish.1 = bf16[9216,128]{1,0:T(8,128)(2,1)} custom-call(bf16[4608,128]{1,0:T(8,128)(2,1)S(1)} %bitcast.22, bf16[4608,128]{1,0:T(8,128)(2,1)S(1)} %bitcast.23, bf16[128,128]{1,0:T(8,128)(2,1)S(1)} %copy-done.2, f32[1,128]{1,0:T(1,128)S(1)} %bitcast.26), custom_call_target="tpu_custom_call" | custom-call | tf_op jit(solution)/shard_map/finish/pallas_call | solution.py:437
  (1 shorter events, 0.0 us)
Async XLA Ops:
  5.2 18.3 %all-to-all-start = ((bf16[8,48,768]{2,1,0:T(8,128)(2,1)}), bf16[8,48,768]{2,1,0:T(8,128)(2,1)S(1)}, u32[]{:S(2)}, u32[]{:S(2)}) async-start(bf16[8,48,768]{2,1,0:T(8,128)(2,1)} %bitcast.29), calls=%async_computation | async-start | bytes 1179648 | tf_op jit(solution)/shard_map/all_to_all | solution.py:142
  23.6 0.8 copy-start
  24.4 20.6 %collective-permute-start.2 = (bf16[384,768]{1,0:T(8,128)(2,1)}, bf16[384,768]{1,0:T(8,128)(2,1)S(1)}, u32[]{:S(2)}, u32[]{:S(2)}) collective-permute-start(bf16[384,768]{1,0:T(8,128)(2,1)} %get-tuple-element.16.refs_0_), channel_id=1, source_target_pairs={{0,12},{2,50},{4,0},{6,54},{8,4},{10,58},{12,8},{14,62},{16,28},{1... | collective-permute-start | bytes 1769480 | tf_op jit(solution)/shard_map/ppermute | solution.py:151
  27.4 17.6 %collective-permute-start.1 = (bf16[384,768]{1,0:T(8,128)(2,1)}, bf16[384,768]{1,0:T(8,128)(2,1)S(1)}, u32[]{:S(2)}, u32[]{:S(2)}) collective-permute-start(bf16[384,768]{1,0:T(8,128)(2,1)} %get-tuple-element.16.refs_0_), channel_id=1, source_target_pairs={{0,8},{2,34},{4,12},{6,38},{8,0},{10,42},{12,4},{14,46},{16,24},{1... | collective-permute-start | bytes 1769480 | tf_op jit(solution)/shard_map/ppermute | solution.py:151
  27.6 22.4 %collective-permute-start = (bf16[384,768]{1,0:T(8,128)(2,1)}, bf16[384,768]{1,0:T(8,128)(2,1)S(1)}, u32[]{:S(2)}, u32[]{:S(2)}) collective-permute-start(bf16[384,768]{1,0:T(8,128)(2,1)} %get-tuple-element.16.refs_0_), channel_id=1, source_target_pairs={{0,4},{2,18},{4,8},{6,22},{8,12},{10,26},{12,0},{14,30},{16,20},{1... | collective-permute-start | bytes 1769480 | tf_op jit(solution)/shard_map/ppermute | solution.py:151
  28.3 9.0 %copy-start.1 = (bf16[384,768]{1,0:T(8,128)(2,1)S(1)}, bf16[384,768]{1,0:T(8,128)(2,1)}, u32[]{:S(2)}) copy-start(bf16[384,768]{1,0:T(8,128)(2,1)} %get-tuple-element.16.refs_0_) | copy-start | bytes 1769476
  28.3 31.9 %all-to-all-start.1 = ((bf16[64,72,128]{2,1,0:T(8,128)(2,1)}), bf16[64,72,128]{2,1,0:T(8,128)(2,1)S(1)}, u32[]{:S(2)}, u32[]{:S(2)}) async-start(bf16[64,72,128]{2,1,0:T(8,128)(2,1)} %bitcast.30), calls=%async_computation.1 | async-start | bytes 2359296 | tf_op jit(solution)/shard_map/all_to_all | solution.py:390
  37.3 15.8 %collective-permute-start.3 = (bf16[384,768]{1,0:T(8,128)(2,1)S(1)}, bf16[384,768]{1,0:T(8,128)(2,1)S(1)}, u32[]{:S(2)}, u32[]{:S(2)}) collective-permute-start(bf16[384,768]{1,0:T(8,128)(2,1)S(1)} %copy-done.1), channel_id=1, source_target_pairs={{0,2},{2,0},{4,6},{6,4},{8,10},{10,8},{12,14},{14,12},{16,18},{18,... | collective-permute-start | bytes 1769480 | tf_op jit(solution)/shard_map/ppermute | solution.py:153
  45.0 8.1 %collective-permute-start.6 = (bf16[384,768]{1,0:T(8,128)(2,1)S(1)}, bf16[384,768]{1,0:T(8,128)(2,1)S(1)}, u32[]{:S(2)}, u32[]{:S(2)}) collective-permute-start(bf16[384,768]{1,0:T(8,128)(2,1)S(1)} %collective-permute-done.2.refs_3_), channel_id=1, source_target_pairs={{0,2},{2,0},{4,6},{6,4},{8,10},{10,8},{12,14},{14,12},{16,18},{18,... | collective-permute-start | bytes 1769480 | tf_op jit(solution)/shard_map/ppermute | solution.py:153
  45.0 8.1 %collective-permute-start.5 = (bf16[384,768]{1,0:T(8,128)(2,1)S(1)}, bf16[384,768]{1,0:T(8,128)(2,1)S(1)}, u32[]{:S(2)}, u32[]{:S(2)}) collective-permute-start(bf16[384,768]{1,0:T(8,128)(2,1)S(1)} %collective-permute-done.1.refs_2_), channel_id=1, source_target_pairs={{0,2},{2,0},{4,6},{6,4},{8,10},{10,8},{12,14},{14,12},{16,18},{18,... | collective-permute-start | bytes 1769480 | tf_op jit(solution)/shard_map/ppermute | solution.py:153
  50.1 4.6 %collective-permute-start.4 = (bf16[384,768]{1,0:T(8,128)(2,1)S(1)}, bf16[384,768]{1,0:T(8,128)(2,1)S(1)}, u32[]{:S(2)}, u32[]{:S(2)}) collective-permute-start(bf16[384,768]{1,0:T(8,128)(2,1)S(1)} %collective-permute-done.refs_1_), channel_id=1, source_target_pairs={{0,2},{2,0},{4,6},{6,4},{8,10},{10,8},{12,14},{14,12},{16,18},{18,... | collective-permute-start | bytes 1769480 | tf_op jit(solution)/shard_map/ppermute | solution.py:153
  60.2 6.7 %copy-start.3 = (f32[128]{0:T(128)S(1)}, f32[128]{0:T(128)}, u32[]{:S(2)}) copy-start(f32[128]{0:T(128)} %param.21) | copy-start | bytes 1540
  60.2 84.2 %all-to-all-start.3 = ((bf16[64,72,128]{2,1,0:T(8,128)(2,1)}), bf16[64,72,128]{2,1,0:T(8,128)(2,1)S(1)}, u32[]{:S(2)}, u32[]{:S(2)}) async-start(bf16[64,72,128]{2,1,0:T(8,128)(2,1)} %bitcast.12), calls=%async_computation.3 | async-start | bytes 2359296 | tf_op jit(solution)/shard_map/all_to_all | solution.py:390
  144.4 86.9 %all-to-all-start.2 = ((bf16[64,72,128]{2,1,0:T(8,128)(2,1)}), bf16[64,72,128]{2,1,0:T(8,128)(2,1)S(1)}, u32[]{:S(2)}, u32[]{:S(2)}) async-start(bf16[64,72,128]{2,1,0:T(8,128)(2,1)} %bitcast.10), calls=%async_computation.2 | async-start | bytes 2359296 | tf_op jit(solution)/shard_map/all_to_all | solution.py:433
  231.3 30.3 %copy-start.2 = (bf16[128,128]{1,0:T(8,128)(2,1)S(1)}, bf16[128,128]{1,0:T(8,128)(2,1)}, u32[]{:S(2)}) copy-start(bf16[128,128]{1,0:T(8,128)(2,1)} %refs_2_.3) | copy-start | bytes 98308
  231.3 30.3 %copy-start.4 = (f32[128]{0:T(128)S(1)}, f32[128]{0:T(128)}, u32[]{:S(2)}) copy-start(f32[128]{0:T(128)} %param.23) | copy-start | bytes 1540
